TPU v7x, 128 devices: a whole 4x4x4 slice. The times are simulated.
128 devices in a mesh: row: 8 (over x, z_hi), col: 16 (over y, z_lo, core).
Axes of the slice: x: 4, y: 4, z: 4 (z_hi: 2, z_lo: 2; z = z_hi * 2 + z_lo), core: 2. Of those that a mesh axis runs over, the one named last changes fastest.
Arguments:
- pair: bfloat16 [1024, 65536], P('row', 'col'), may hold values from -6 to 6
- tile_mask: int32 [16, 16], replicated, may hold values from 0 to 1, as said below
- w_first: bfloat16 [3, 3, 64, 64], replicated, may hold values from -0.25 to 0.25
- b_first: float32 [64], replicated, may hold values from -3 to 3
- w_second: bfloat16 [3, 3, 64, 64], replicated, may hold values from -0.25 to 0.25
- b_second: float32 [64], replicated, may hold values from -3 to 3
- norm_gain: float32 [64], replicated, may hold values from 0.5 to 1.5
- w_proj: bfloat16 [64, 384], replicated, may hold values from -0.75 to 0.75
Outputs:
- update: bfloat16 [1024, 384], P(('row', 'col'))
Inputs may be any that keep to these rules, and one draw needn't show every extreme that they name: tile_mask is symmetric and its diagonal is 1; it is constant on blocks of tiles that belong to one pair of chains.
All inputs are finite; a program needn't handle non-finite values.
Results may differ from a plain program's by a relative error of at most 0.015.
Values may be sent and summed in bfloat16 or wider, within the bound.
A program may use at most 64 MiB of HBM per device.

v0:
```python
import jax
import jax.numpy as jnp
from jax import lax
from jax.sharding import PartitionSpec as P

TILE = 64


EPSILON = 1e-05


def with_halo(cells, sides, width):
    for axis, dim in sides:
        count = lax.axis_size(axis)
        ends = count - 1
        head = lax.slice_in_dim(cells, 0, width, axis=dim)
        tail = lax.slice_in_dim(cells, cells.shape[dim] - width, cells.shape[dim], axis=dim)
        cells = jnp.concatenate(
            [
                lax.ppermute(tail, axis, [(i, (i + 1) % count) for i in range(ends)]),
                cells,
                lax.ppermute(head, axis, [((i + 1) % count, i) for i in range(ends)]),
            ],
            axis=dim,
        )
    return cells


def packed_kernel(weight, channels):
    doubled = jnp.zeros((3, 3, 2 * channels, 2 * channels), jnp.bfloat16)
    doubled = doubled.at[:, :, :channels, :channels].set(weight)
    return doubled.at[:, :, channels:, channels:].set(weight)


def apply_taps(window, kernel, dilation, height, width):
    result = jnp.zeros((height, width, kernel.shape[3]), jnp.float32)
    for tap_row in range(3):
        for tap_col in range(3):
            row_start = tap_row * dilation
            col_start = tap_col * (dilation // 2)
            piece = window[row_start : row_start + height, col_start : col_start + width]
            result = result + jnp.einsum(
                "rcx,xy->rcy", piece, kernel[tap_row, tap_col], preferred_element_type=jnp.float32
            )
    return result


def with_rims(field, dilation):
    row_count, half_cols, packed = field.shape
    paired = field.reshape(row_count // 2, 2, half_cols, packed)
    grown = with_halo(paired, (("row", 0), ("col", 2)), dilation // 2)
    return grown.reshape(row_count + 2 * dilation, half_cols + dilation, packed)


def conv_padded(padded, kernel, dilation, row_count, half_cols):
    return apply_taps(padded, kernel, dilation, row_count, half_cols)


def body(pair, tile_mask, w_first, b_first, w_second, b_second, norm_gain, w_proj):
    channels = w_first.shape[2]
    packed = 2 * channels
    row_count = pair.shape[0]
    col_count = pair.shape[1] // channels
    half_cols = col_count // 2
    row_at = lax.axis_index("row")
    col_at = lax.axis_index("col")
    tile_rows = row_count // TILE
    tile_cols = col_count // TILE
    live_tiles = lax.dynamic_slice(
        tile_mask, (row_at * tile_rows, col_at * tile_cols), (tile_rows, tile_cols)
    ).astype(jnp.float32)
    cell_live = jnp.broadcast_to(
        live_tiles[:, None, :, None, None], (tile_rows, TILE, tile_cols, TILE // 2, 2)
    ).reshape(row_count, half_cols, 2)

    def masked(values):
        return (values.reshape(row_count, half_cols, 2, channels) * cell_live[..., None]).reshape(
            row_count, half_cols, packed
        )

    inputs = pair.reshape(row_count, half_cols, packed)
    kernel_one = packed_kernel(w_first, channels)
    kernel_two = packed_kernel(w_second, channels)
    bias_one = jnp.concatenate([b_first, b_first])
    bias_two = jnp.concatenate([b_second, b_second])
    first_out = conv_padded(with_rims(inputs, 2), kernel_one, 2, row_count, half_cols) + bias_one
    hidden = masked(jax.nn.elu(first_out)).astype(jnp.bfloat16)
    second_out = conv_padded(with_rims(hidden, 4), kernel_two, 4, row_count, half_cols) + bias_two
    result = masked(inputs.astype(jnp.float32) + second_out).astype(jnp.bfloat16)
    total_rows = col_count * lax.axis_size("col")
    cells = result.reshape(row_count, col_count, channels)
    row_part = jnp.sum(cells, axis=1, dtype=jnp.float32)
    col_part = jnp.sum(cells, axis=0, dtype=jnp.float32)
    blank = jnp.zeros((total_rows, channels), jnp.float32)
    contrib = lax.dynamic_update_slice(blank, row_part, (row_at * row_count, 0))
    contrib = contrib + lax.dynamic_update_slice(blank, col_part, (col_at * col_count, 0))
    pooled = lax.psum_scatter(contrib, ("row", "col"), scatter_dimension=0, tiled=True)
    center = jnp.mean(pooled, axis=1, keepdims=True)
    spread = jnp.mean((pooled - center) ** 2, axis=1, keepdims=True)
    normed = ((pooled - center) / jnp.sqrt(spread + EPSILON) * norm_gain).astype(jnp.bfloat16)
    return jnp.dot(normed, w_proj, preferred_element_type=jnp.float32).astype(jnp.bfloat16)


def solution(mesh):
    return jax.shard_map(
        body,
        mesh=mesh,
        in_specs=(P("row", "col"), P(), P(), P(), P(), P(), P(), P()),
        out_specs=P(("row", "col"), None),
        check_vma=False,
    )
```

profile of v0, /device:TPU:1, one launch (start us, length us, event | category | flops | bytes accessed | tf_op | source)
XLA Modules:
  0.0 238.8 jit_solution(4108425200894896357)
XLA Ops:
  6.5 0.9 slice_bitcast_fusion.36
  7.5 6.3 %collective-permute-start = (bf16[1,2,32,128]{3,1,0,2:T(2,128)(2,1)S(1)}, bf16[1,2,32,128]{3,1,0,2:T(2,128)(2,1)S(1)}, u32[]{:S(2)}, u32[]{:S(2)}) collective-permute-start(bf16[1,2,32,128]{3,1,0,2:T(2,128)(2,1)S(1)} %get-tuple-element.60), channel_id=1, source_target_pairs={{0,16},{16,32},{32,48},{48,64},{64,80},{80,96},{96,112},{1,17},{17... | collective-permute-start | bytes 49160 | tf_op jit(solution)/shard_map/ppermute | solution.py:20
  13.8 1.3 collective-permute-start.1
  15.1 1.5 copy.67
  16.7 1.1 copy_dynamic-update-slice_fusion
  17.8 2.0 collective-permute-done.1
  19.9 4.6 %collective-permute-start.2 = (bf16[66,2,1,128]{3,1,0,2:T(2,128)(2,1)S(1)}, bf16[66,2,1,128]{3,1,0,2:T(2,128)(2,1)S(1)}, u32[]{:S(2)}, u32[]{:S(2)}) collective-permute-start(bf16[66,2,1,128]{3,1,0,2:T(2,128)(2,1)S(1)} %get-tuple-element.55), channel_id=1, source_target_pairs={{0,1},{1,2},{2,3},{3,4},{4,5},{5,6},{6,7},{7,8},{8,9},{9,10},{10,1... | collective-permute-start | bytes 101384 | tf_op jit(solution)/shard_map/ppermute | solution.py:20
  24.5 1.9 collective-permute-start.3
  26.5 0.9 convert_reduce_fusion
  27.6 4.1 %scatter.15 = bf16[3,3,128,128]{3,2,1,0:T(8,128)(2,1)S(1)} dynamic-update-slice(bf16[3,3,128,128]{3,2,1,0:T(8,128)(2,1)S(1)} %scatter.14, bf16[3,3,64,64]{3,2,1,0:T(8,128)(2,1)S(1)} %copy-done.6, s32[]{:T(128)} %constant.123.clone.1, s32[]{:T(128)} %constant.123.clone.1, s32[]{:T(128)} %constant.124.clone.1, s32[]{:T(128)} %constant.124.clone.1) | dynamic-update-slice | bytes 147460 | tf_op jit(solution)/shard_map/scatter | solution.py:32
  31.7 0.7 copy-done.4
  32.4 1.8 pad_maximum_fusion.1
  34.2 1.7 reshape.192
  39.4 2.7 %fusion.2 = bf16[128,32,128]{2,0,1:T(8,128)(2,1)S(1)} fusion(f32[128,32,128]{2,0,1:T(8,128)S(1)} %fusion.22, f32[128,32,128]{2,0,1:T(8,128)S(1)} %fusion.24, f32[128,32,128]{2,0,1:T(8,128)S(1)} %fusion.26, f32[128,32,128]{2,0,1:T(8,128)S(1)} %fusion.28, f32[128,32,128]{2,0,1:T(8,128)S(1)} %fusion.30, f32[128,32,128]{2,0,1:T(8,128)S(1)} %fusion.32, ...), kind=kOutput, calls=%fused_computation.4 | convolution fusion | flops 141557760 | bytes 18908160 | tf_op jit(solution)/shard_map/rcx,xy->rcy/dot_general | solution.py:42
  42.8 4.6 %collective-permute-start.4 = (bf16[2,2,32,128]{3,1,0,2:T(2,128)(2,1)}, bf16[2,2,32,128]{3,1,0,2:T(2,128)(2,1)S(1)}, u32[]{:S(2)}, u32[]{:S(2)}) collective-permute-start(bf16[2,2,32,128]{3,1,0,2:T(2,128)(2,1)} %bitcast.21), channel_id=1, source_target_pairs={{0,16},{16,32},{32,48},{48,64},{64,80},{80,96},{96,112},{1,17},{17... | collective-permute-start | bytes 98312 | tf_op jit(solution)/shard_map/ppermute | solution.py:20
  47.4 1.3 collective-permute-start.5
  48.7 0.7 copy.40
  49.6 4.1 %scatter.19 = bf16[3,3,128,128]{2,3,1,0:T(8,128)(2,1)S(1)} dynamic-update-slice(bf16[3,3,128,128]{2,3,1,0:T(8,128)(2,1)S(1)} %scatter.16, bf16[3,3,64,64]{2,3,1,0:T(8,128)(2,1)S(1)} %copy.44, s32[]{:T(128)} %constant.123.clone.1, s32[]{:T(128)} %constant.123.clone.1, s32[]{:T(128)} %constant.124.clone.1, s32[]{:T(128)} %constant.124.clone.1) | dynamic-update-slice | bytes 147460 | tf_op jit(solution)/shard_map/scatter | solution.py:32
  53.7 1.6 copy.55
  55.6 3.3 %collective-permute-start.6 = (bf16[68,2,2,128]{3,1,0,2:T(2,128)(2,1)S(1)}, bf16[68,2,2,128]{3,1,0,2:T(2,128)(2,1)S(1)}, u32[]{:S(2)}, u32[]{:S(2)}) collective-permute-start(bf16[68,2,2,128]{3,1,0,2:T(2,128)(2,1)S(1)} %get-tuple-element.53), channel_id=1, source_target_pairs={{0,1},{1,2},{2,3},{3,4},{4,5},{5,6},{6,7},{7,8},{8,9},{9,10},{10,1... | collective-permute-start | bytes 208904 | tf_op jit(solution)/shard_map/ppermute | solution.py:20
  58.9 2.1 collective-permute-start.7
  61.1 3.4 %collective-permute-done.7 = bf16[68,2,2,128]{3,1,0,2:T(2,128)(2,1)S(1)} collective-permute-done((bf16[68,2,2,128]{3,1,0,2:T(2,128)(2,1)S(1)}, bf16[68,2,2,128]{3,1,0,2:T(2,128)(2,1)S(1)}, u32[]{:S(2)}, u32[]{:S(2)}) %collective-permute-start.7) | collective-permute-done | bytes 69664 | tf_op jit(solution)/shard_map/ppermute | solution.py:22
  64.5 4.2 %pad_maximum_fusion = bf16[68,2,36,128]{3,1,0,2:T(2,128)(2,1)S(1)} fusion(bf16[68,2,2,128]{3,1,0,2:T(2,128)(2,1)S(1)} %collective-permute-done.7, bf16[2,2,32,128]{3,1,0,2:T(2,128)(2,1)S(1)} %collective-permute-done.5, bf16[64,2,32,128]{3,1,0,2:T(2,128)(2,1)S(1)} %bitcast.119, bf16[2,2,32,128]{3,1,0,2:T(2,128)(2,1)S(1)} %collective-permute-done.4, ...), kind=kLoop, calls=%fused_computation.7 | loop fusion | flops 2506752 | bytes 2506752 | tf_op jit(solution)/shard_map/concatenate | solution.py:18
  72.3 1.1 copy-done.1
  73.5 1.2 fusion.44
  74.6 1.9 copy.56
  76.5 1.7 reduce_sum.38
  78.5 0.8 copy-done.3
  79.3 149.5 %all-reduce.5.cloned.1.call-done = f32[1024,64]{1,0:T(8,128)} async-done(((f32[1024,64]{1,0:T(8,128)}), f32[1024,64]{1,0:T(8,128)}) %all-reduce.5.cloned.1.call-update) | async-done | bytes 262160
  228.8 0.8 dynamic-slice_reduce_fusion
  229.6 0.9 multiply_reduce_fusion
  230.5 1.5 convolution_convert_fusion
  (62 shorter events, 8.8 us)
Async XLA Ops:
  6.5 223.9 %copy-start = (bf16[64,384]{1,0:T(8,128)(2,1)S(1)}, bf16[64,384]{1,0:T(8,128)(2,1)}, u32[]{:S(2)}) copy-start(bf16[64,384]{1,0:T(8,128)(2,1)} %param.23) | copy-start | bytes 147460
  6.5 222.2 %all-reduce.5.cloned.1.call-start = ((), (), s32[]{:S(2)}) async-start(), calls=%async_computation | async-start | bytes 1048576
  7.5 9.2 %collective-permute-start = (bf16[1,2,32,128]{3,1,0,2:T(2,128)(2,1)S(1)}, bf16[1,2,32,128]{3,1,0,2:T(2,128)(2,1)S(1)}, u32[]{:S(2)}, u32[]{:S(2)}) collective-permute-start(bf16[1,2,32,128]{3,1,0,2:T(2,128)(2,1)S(1)} %get-tuple-element.60), channel_id=1, source_target_pairs={{0,16},{16,32},{32,48},{48,64},{64,80},{80,96},{96,112},{1,17},{17... | collective-permute-start | bytes 49160 | tf_op jit(solution)/shard_map/ppermute | solution.py:20
  13.8 6.0 %collective-permute-start.1 = (bf16[1,2,32,128]{3,1,0,2:T(2,128)(2,1)S(1)}, bf16[1,2,32,128]{3,1,0,2:T(2,128)(2,1)S(1)}, u32[]{:S(2)}, u32[]{:S(2)}) collective-permute-start(bf16[1,2,32,128]{3,1,0,2:T(2,128)(2,1)S(1)} %get-tuple-element.59), channel_id=1, source_target_pairs={{16,0},{32,16},{48,32},{64,48},{80,64},{96,80},{112,96},{17,1},{33... | collective-permute-start | bytes 49160 | tf_op jit(solution)/shard_map/ppermute | solution.py:22
  15.1 11.3 %copy-start.8 = (f32[64]{0:T(128)S(1)}, f32[64]{0:T(128)}, u32[]{:S(2)}) copy-start(f32[64]{0:T(128)} %param.19) | copy-start | bytes 772
  15.1 12.5 %copy-start.6 = (bf16[3,3,64,64]{3,2,1,0:T(8,128)(2,1)S(1)}, bf16[3,3,64,64]{3,2,1,0:T(8,128)(2,1)}, u32[]{:S(2)}) copy-start(bf16[3,3,64,64]{3,2,1,0:T(8,128)(2,1)} %param.18) | copy-start | bytes 221188
  19.9 11.9 %collective-permute-start.2 = (bf16[66,2,1,128]{3,1,0,2:T(2,128)(2,1)S(1)}, bf16[66,2,1,128]{3,1,0,2:T(2,128)(2,1)S(1)}, u32[]{:S(2)}, u32[]{:S(2)}) collective-permute-start(bf16[66,2,1,128]{3,1,0,2:T(2,128)(2,1)S(1)} %get-tuple-element.55), channel_id=1, source_target_pairs={{0,1},{1,2},{2,3},{3,4},{4,5},{5,6},{6,7},{7,8},{8,9},{9,10},{10,1... | collective-permute-start | bytes 101384 | tf_op jit(solution)/shard_map/ppermute | solution.py:20
  24.5 7.2 %collective-permute-start.3 = (bf16[66,2,1,128]{3,1,0,2:T(2,128)(2,1)S(1)}, bf16[66,2,1,128]{3,1,0,2:T(2,128)(2,1)S(1)}, u32[]{:S(2)}, u32[]{:S(2)}) collective-permute-start(bf16[66,2,1,128]{3,1,0,2:T(2,128)(2,1)S(1)} %get-tuple-element.56), channel_id=1, source_target_pairs={{1,0},{2,1},{3,2},{4,3},{5,4},{6,5},{7,6},{8,7},{9,8},{10,9},{11,1... | collective-permute-start | bytes 101384 | tf_op jit(solution)/shard_map/ppermute | solution.py:22
  31.7 0.7 copy-start.4
  34.2 1.8 copy-start.5
  39.4 9.3 %copy-start.2 = (bf16[128,4096]{1,0:T(8,128)(2,1)S(1)}, bf16[128,4096]{1,0:T(8,128)(2,1)}, u32[]{:S(2)}) copy-start(bf16[128,4096]{1,0:T(8,128)(2,1)} %param.16) | copy-start | bytes 3145732
  42.2 7.3 %copy-start.7 = (bf16[3,3,64,64]{3,2,1,0:T(8,128)(2,1)S(1)}, bf16[3,3,64,64]{3,2,1,0:T(8,128)(2,1)}, u32[]{:S(2)}) copy-start(bf16[3,3,64,64]{3,2,1,0:T(8,128)(2,1)} %param.20) | copy-start | bytes 221188
  42.8 12.6 %collective-permute-start.4 = (bf16[2,2,32,128]{3,1,0,2:T(2,128)(2,1)}, bf16[2,2,32,128]{3,1,0,2:T(2,128)(2,1)S(1)}, u32[]{:S(2)}, u32[]{:S(2)}) collective-permute-start(bf16[2,2,32,128]{3,1,0,2:T(2,128)(2,1)} %bitcast.21), channel_id=1, source_target_pairs={{0,16},{16,32},{32,48},{48,64},{64,80},{80,96},{96,112},{1,17},{17... | collective-permute-start | bytes 98312 | tf_op jit(solution)/shard_map/ppermute | solution.py:20
  47.4 8.0 %collective-permute-start.5 = (bf16[2,2,32,128]{3,1,0,2:T(2,128)(2,1)}, bf16[2,2,32,128]{3,1,0,2:T(2,128)(2,1)S(1)}, u32[]{:S(2)}, u32[]{:S(2)}) collective-permute-start(bf16[2,2,32,128]{3,1,0,2:T(2,128)(2,1)} %bitcast.23), channel_id=1, source_target_pairs={{16,0},{32,16},{48,32},{64,48},{80,64},{96,80},{112,96},{17,1},{33... | collective-permute-start | bytes 98312 | tf_op jit(solution)/shard_map/ppermute | solution.py:22
  53.7 7.3 %copy-start.9 = (f32[64]{0:T(128)S(1)}, f32[64]{0:T(128)}, u32[]{:S(2)}) copy-start(f32[64]{0:T(128)} %param.21) | copy-start | bytes 772
  55.6 5.5 %collective-permute-start.6 = (bf16[68,2,2,128]{3,1,0,2:T(2,128)(2,1)S(1)}, bf16[68,2,2,128]{3,1,0,2:T(2,128)(2,1)S(1)}, u32[]{:S(2)}, u32[]{:S(2)}) collective-permute-start(bf16[68,2,2,128]{3,1,0,2:T(2,128)(2,1)S(1)} %get-tuple-element.53), channel_id=1, source_target_pairs={{0,1},{1,2},{2,3},{3,4},{4,5},{5,6},{6,7},{7,8},{8,9},{9,10},{10,1... | collective-permute-start | bytes 208904 | tf_op jit(solution)/shard_map/ppermute | solution.py:20
  58.9 5.6 %collective-permute-start.7 = (bf16[68,2,2,128]{3,1,0,2:T(2,128)(2,1)S(1)}, bf16[68,2,2,128]{3,1,0,2:T(2,128)(2,1)S(1)}, u32[]{:S(2)}, u32[]{:S(2)}) collective-permute-start(bf16[68,2,2,128]{3,1,0,2:T(2,128)(2,1)S(1)} %get-tuple-element.54), channel_id=1, source_target_pairs={{1,0},{2,1},{3,2},{4,3},{5,4},{6,5},{7,6},{8,7},{9,8},{10,9},{11,1... | collective-permute-start | bytes 208904 | tf_op jit(solution)/shard_map/ppermute | solution.py:22
  71.9 1.6 copy-start.1
  76.5 154.0 %copy-start.10 = (f32[64]{0:T(128)S(1)}, f32[64]{0:T(128)}, u32[]{:S(2)}) copy-start(f32[64]{0:T(128)} %param.22) | copy-start | bytes 772
  78.5 0.8 copy-start.3
Sparse Core Ops, SparseCore 0:
  79.4 149.2 all-reduce.4
where the time goes:
time: 239 us
  waiting for transfers between devices  155 us (65%)
  starting transfers between devices  25.5 us (11%)
  local copies, waits for them, and re-layouts  21.6 us (9%)
  between operations  13.8 us (6%)
  matrix products  12.3 us (5%)
  other arithmetic  10.7 us (4%)
    unnamed x2, waiting for transfers between devices  149 us
    ppermute x4, starting transfers between devices, with_halo(): lax.ppermute(tail, axis, [(i, (i + 1) % count) for i in range(ends)])  18.9 us
    dot_general x18, matrix products, apply_taps(): jnp.einsum('rcx,xy->rcy', piece, kernel[tap_row, tap_col], preferred_elem...  10.8 us
    scatter x2, local copies, waits for them, and re-layouts, packed_kernel(): return doubled.at[:, :, channels:, channels:].set(weight)  8.18 us
    ppermute x4, starting transfers between devices, with_halo(): lax.ppermute(head, axis, [((i + 1) % count, i) for i in range(ends)])  6.61 us
    unnamed x27, local copies, waits for them, and re-layouts  6.11 us
    concatenate x2, other arithmetic, with_halo(): jnp.concatenate([lax.ppermute(tail, axis, [(i, (i + 1) % count) for i in...  5.99 us
    ppermute x4, waiting for transfers between devices, with_halo(): lax.ppermute(head, axis, [((i + 1) % count, i) for i in range(ends)])  5.42 us
  transfers between devices with their start and end apart: 9, of which 3 were waited for; matrix products, arithmetic and copies ran while one was open for 6% of the time, Pallas kernels for 0%

commit v1 on v0

v1 whole, which is shorter than its diff:
```python
import functools

import jax
import jax.numpy as jnp
from jax import lax
from jax.experimental import pallas as pl
from jax.experimental.pallas import tpu as pltpu
from jax.sharding import PartitionSpec as P

TILE = 64
EPSILON = 1e-05
MESH = pl.DeviceIdType.MESH
F32 = jnp.float32
BF16 = jnp.bfloat16

ROWS = 128
PAIRS = 32
EDGE = 16
GROUPS = 16
OWN = 128
LANES = PAIRS * 128


def elu(v):
    return jnp.where(v > 0, v, jnp.exp(jnp.minimum(v, 0.0)) - 1.0)


def kernel(
    n_row, n_col,
    pair, mask, w1, b1, w2, b2, gain, wp,
    out,
    xe, xm, xp, hb, wt1, wt2, bias, hs, xs, racc, cacc, csum, rsend, csend, rrecv, crecv, total, res,
    load_sem, halo_send, halo_recv, row_send, row_recv, col_send, col_recv,
):
    r = lax.axis_index("row")
    c = lax.axis_index("col")
    me = r * n_col + c
    n_all = n_row * n_col

    load = pltpu.make_async_copy(pair, xe.at[pl.ds(EDGE, ROWS), pl.ds(OWN, LANES)], load_sem)
    load.start()

    barrier = pltpu.get_barrier_semaphore()

    def greet(tr, tc):
        same = jnp.logical_and(tr == r, tc == c)

        @pl.when(jnp.logical_not(same))
        def _():
            pl.semaphore_signal(barrier, inc=1, device_id=(tr, tc), device_id_type=MESH)

    up, down = lax.rem(r + n_row - 1, n_row), lax.rem(r + 1, n_row)
    left, right = lax.rem(c + n_col - 1, n_col), lax.rem(c + 1, n_col)
    top, bottom = pl.ds(0, EDGE), pl.ds(ROWS - EDGE, EDGE)
    first, last = pl.ds(0, 128), pl.ds(LANES - 128, 128)
    above, below, whole = pl.ds(0, EDGE), pl.ds(EDGE + ROWS, EDGE), pl.ds(EDGE, ROWS)
    before, after, inside = pl.ds(0, 128), pl.ds(OWN + LANES, 128), pl.ds(OWN, LANES)
    every, every_row = pl.ds(0, LANES), pl.ds(0, ROWS)
    halos = [
        (up, c, top, every, below, inside),
        (down, c, bottom, every, above, inside),
        (r, left, every_row, first, whole, after),
        (r, right, every_row, last, whole, before),
        (up, left, top, first, below, after),
        (up, right, top, last, below, before),
        (down, left, bottom, first, above, after),
        (down, right, bottom, last, above, before),
    ]
    for halo in halos:
        pl.semaphore_signal(barrier, inc=1, device_id=(halo[0], halo[1]), device_id_type=MESH)

    @pl.loop(1, n_col)
    def _(k):
        pl.semaphore_signal(
            barrier, inc=1, device_id=(r, lax.rem(c + k, n_col)), device_id_type=MESH
        )

    for edge, other in ((0, up), (n_col - 1, down)):
        @pl.when(c == edge)
        def _():
            @pl.loop(0, n_col)
            def _(k):
                pl.semaphore_signal(barrier, inc=1, device_id=(other, k), device_id_type=MESH)

    block = me // 8
    part = lax.rem(me, 8)

    @pl.loop(0, n_row)
    def _(k):
        greet(k, block)

    for edge, step in ((0, n_col - 1), (7, 1)):
        @pl.when(part == edge)
        def _():
            @pl.loop(0, n_row)
            def _(k):
                greet(k, lax.rem(block + step, n_col))

    zero = jnp.zeros((64, 64), BF16)
    wt1[...] = jnp.zeros_like(wt1)
    for a in range(3):
        for b in range(3):
            w = w1[a, b]
            doubled = jnp.concatenate(
                [jnp.concatenate([w, zero], axis=1), jnp.concatenate([zero, w], axis=1)], axis=0
            )
            for n in range(2):
                wt1[pl.ds(a * 512 + (b + n) * 128, 128), pl.ds(n * 128, 128)] = doubled
            w = w2[a, b]
            wt2[pl.ds((a * 3 + b) * 128, 128), :] = jnp.concatenate(
                [jnp.concatenate([w, zero], axis=1), jnp.concatenate([zero, w], axis=1)], axis=0
            )
    bias_one = jnp.concatenate([b1[...]] * 4, axis=1)
    bias_two = jnp.concatenate([b2[...]] * 2, axis=1)

    def tile(t, v):
        ti = 2 * r - 1 + t
        tj = c + v
        ok = (ti >= 0) & (ti < 2 * n_row) & (tj >= 0) & (tj < n_col)
        value = mask[jnp.clip(ti, 0, 2 * n_row - 1), jnp.clip(tj, 0, n_col - 1)]
        return jnp.where(ok, value, 0).astype(F32)

    mt = [[tile(t, v) for v in (0, -1, 1)] for t in range(4)]

    def by_row(rows, v):
        return jnp.where(
            rows < 0, mt[0][v], jnp.where(rows < 64, mt[1][v], jnp.where(rows < 128, mt[2][v], mt[3][v]))
        )

    to_self = lax.rem(me - 8 * c + 1 + n_all, n_all) < 10
    pl.semaphore_wait(barrier, 8 + (n_col - 1) + 2 + 10 - jnp.where(to_self, 1, 0))
    copies = []
    for k, (tr, tc, src_rows, src_lanes, dst_rows, dst_lanes) in enumerate(halos):
        copy = pltpu.make_async_remote_copy(
            src_ref=pair.at[src_rows, src_lanes],
            dst_ref=xe.at[dst_rows, dst_lanes],
            send_sem=halo_send.at[k],
            recv_sem=halo_recv.at[k],
            device_id=(tr, tc),
            device_id_type=MESH,
        )
        copy.start()
        copies.append(copy)

    load.wait()

    def shift(r0, lanes):
        window = xe[pl.ds(r0, 48), lanes]
        xm[pl.ds(r0, 16), lanes] = window[14:30]
        xp[pl.ds(r0, 16), lanes] = window[18:34]

    def taps(r0, rows, g):
        lanes = pl.ds(g * 256, 512)
        return jnp.concatenate(
            [xm[pl.ds(r0, rows), lanes], xe[pl.ds(EDGE + r0, rows), lanes], xp[pl.ds(r0, rows), lanes]],
            axis=1,
        )

    def hidden(r0, rows, groups):
        lhs = jnp.concatenate([taps(r0, rows, g) for g in groups], axis=0)
        h = elu(jnp.dot(lhs, wt1[...], preferred_element_type=F32) + bias_one)
        parts = [h[k * rows : (k + 1) * rows] for k in range(len(groups))]
        for g, piece in zip(groups, parts):
            hb[pl.ds(r0, rows), pl.ds(g * 256, 256)] = piece.astype(BF16)
        return parts

    def fold(parts):
        both = functools.reduce(jnp.add, parts)
        return both[:, :128] + both[:, 128:]

    def sum_x(r0):
        cells = xe[pl.ds(EDGE + r0, 16), pl.ds(OWN, LANES)].astype(F32)
        xs[pl.ds(r0, 16), :] = functools.reduce(
            jnp.add, [cells[:, p * 128 : (p + 1) * 128] for p in range(PAIRS)]
        )

    @pl.loop(0, 6)
    def _(k):
        r0 = pl.multiple_of(16 + 16 * k, 16)
        shift(r0, pl.ds(OWN, LANES))
        hs[1, pl.ds(r0, 16), :] = fold(hidden(r0, 16, range(1, GROUPS - 1)))
        sum_x(r0)

    for copy in copies:
        copy.wait()

    @pl.when(r == 0)
    def _():
        xe[above, :] = jnp.zeros((EDGE, xe.shape[1]), BF16)

    @pl.when(r == n_row - 1)
    def _():
        xe[below, :] = jnp.zeros((EDGE, xe.shape[1]), BF16)

    @pl.when(c == 0)
    def _():
        xe[:, before] = jnp.zeros((xe.shape[0], 128), BF16)

    @pl.when(c == n_col - 1)
    def _():
        xe[:, after] = jnp.zeros((xe.shape[0], 128), BF16)

    for r0 in range(16, ROWS - 16, 16):
        shift(r0, before)
        shift(r0, after)

    @pl.loop(0, 2)
    def _(k):
        r0 = pl.multiple_of((ROWS - 16) * k, 16)
        shift(r0, pl.ds(0, xe.shape[1]))
        parts = hidden(r0, 16, range(GROUPS))
        hs[0, pl.ds(r0, 16), :] = fold(parts[:1])
        hs[1, pl.ds(r0, 16), :] = fold(parts[1:-1])
        hs[2, pl.ds(r0, 16), :] = fold(parts[-1:])
        sum_x(r0)

    parts = hidden(16, ROWS - 32, (0, GROUPS - 1))
    hs[0, pl.ds(16, ROWS - 32), :] = fold(parts[:1])
    hs[2, pl.ds(16, ROWS - 32), :] = fold(parts[1:])

    def split(values):
        high = values.astype(BF16)
        return jnp.concatenate([high, (values - high.astype(F32)).astype(BF16)], axis=0)

    rows = lax.broadcasted_iota(jnp.int32, (ROWS, 128), 0)
    own = by_row(rows, 0)
    sum_l, sum_m, sum_r = (hs[k] * own for k in range(3))
    racc[...] = jnp.zeros_like(racc)
    racc[pl.ds(8, ROWS), :] = (xs[...] + 32.0 * bias_two) * own
    for a in range(3):
        out_rows = rows - 4 * (a - 1)
        m0, ml, mr = (by_row(out_rows, v) for v in range(3))
        lhs = split(
            jnp.concatenate(
                [
                    m0 * (sum_l + sum_m) + mr * sum_r,
                    m0 * (sum_l + sum_m + sum_r),
                    m0 * (sum_m + sum_r) + ml * sum_l,
                ],
                axis=1,
            )
        )
        both = jnp.dot(lhs, wt2[pl.ds(a * 384, 384), :], preferred_element_type=F32)
        racc[pl.ds(8 - 4 * (a - 1), ROWS), :] += both[:ROWS] + both[ROWS:]
    racc[...] = racc[...] + pltpu.roll(racc[...], 64, 1)
    half = lax.broadcasted_iota(jnp.int32, (72, 128), 1) < 64
    paired = jnp.where(half, racc[pl.ds(0, 72, stride=2), :], racc[pl.ds(1, 72, stride=2), :])
    for k in range(18):
        rsend[k] = paired[4 * k : 4 * k + 4]

    @pl.loop(0, 18)
    def _(k):
        target = lax.rem(me - c - 1 + k + n_all, n_all)
        slot = jnp.where((k == 0) | (k == 17), n_col + c, c)

        @pl.when(target == me)
        def _():
            pltpu.make_async_copy(rsend.at[k], rrecv.at[slot], row_recv.at[slot]).start()

        @pl.when(target != me)
        def _():
            pltpu.make_async_remote_copy(
                src_ref=rsend.at[k], dst_ref=rrecv.at[slot], send_sem=row_send.at[k],
                recv_sem=row_recv.at[slot], device_id=(target // n_col, lax.rem(target, n_col)),
                device_id_type=MESH,
            ).start()

    combos = [(a, v) for a in range(3) for v in range(3)]
    at = lax.broadcasted_iota(jnp.int32, (16, 128), 1)
    which = lax.broadcasted_iota(jnp.int32, (16, 128), 0)
    own_at = by_row(at, 0)
    pick = jnp.zeros((16, 128), F32)
    for k, (a, v) in enumerate(combos):
        pick = jnp.where(which == k, by_row(at - 4 * (a - 1), v), pick)
    pick = jnp.concatenate([pick * own_at, jnp.where(which == 9, own_at, 0.0)], axis=1).astype(BF16)
    for g in range(GROUPS):
        cells = jnp.concatenate(
            [hb[:, pl.ds(g * 256, 256)], xe[pl.ds(EDGE, ROWS), pl.ds(OWN + g * 256, 256)]], axis=0
        )
        sums = jnp.dot(pick, cells, preferred_element_type=F32)
        csum[pl.ds(g * 32, 16), :] = sums[:, :128]
        csum[pl.ds(g * 32 + 16, 16), :] = sums[:, 128:]

    def column(k):
        return csum[pl.ds(k, PAIRS, stride=16), :]

    at_pair = lax.broadcasted_iota(jnp.int32, (PAIRS, 128), 0)
    cacc[...] = jnp.zeros_like(cacc)
    cacc[pl.ds(8, PAIRS), :] = column(9) + bias_two * (64.0 * (mt[1][0] + mt[2][0]))
    for b in range(3):
        pieces = []
        for a in range(3):
            value = column(3 * a)
            if b == 0:
                value = jnp.where(at_pair >= PAIRS - 2, column(3 * a + 2), value)
            if b == 2:
                value = jnp.where(at_pair < 2, column(3 * a + 1), value)
            pieces.append(value)
        weights = jnp.concatenate([wt2[pl.ds((a * 3 + b) * 128, 128), :] for a in range(3)], axis=0)
        both = jnp.dot(split(jnp.concatenate(pieces, axis=1)), weights, preferred_element_type=F32)
        cacc[pl.ds(8 - 2 * (b - 1), PAIRS), :] += both[:PAIRS] + both[PAIRS:]
    columns = cacc[pl.ds(4, 40), :]
    for k in range(10):
        csend[k] = columns[4 * k : 4 * k + 4]

    @pl.loop(0, 10)
    def _(k):
        target = lax.rem(8 * c - 1 + k + n_all, n_all)
        slot = jnp.where((k == 0) | (k == 9), n_row + r, r)

        @pl.when(target == me)
        def _():
            pltpu.make_async_copy(csend.at[k], crecv.at[slot], col_recv.at[slot]).start()

        @pl.when(target != me)
        def _():
            pltpu.make_async_remote_copy(
                src_ref=csend.at[k], dst_ref=crecv.at[slot], send_sem=col_send.at[k],
                recv_sem=col_recv.at[slot], device_id=(target // n_col, lax.rem(target, n_col)),
                device_id_type=MESH,
            ).start()

    def arrived(buffer, sem, first_slot, count):
        for k in range(first_slot, first_slot + count):
            pltpu.make_async_copy(buffer.at[k], buffer.at[k], sem.at[k]).wait()
        return jnp.sum(buffer[pl.ds(first_slot, count)], axis=0)

    total[...] = arrived(rrecv, row_recv, 0, n_col) + arrived(crecv, col_recv, 0, n_row)

    @pl.when((c == 0) | (c == n_col - 1))
    def _():
        total[...] += arrived(rrecv, row_recv, n_col, n_col)

    @pl.when((part == 0) | (part == 7))
    def _():
        total[...] += arrived(crecv, col_recv, n_row, n_row)

    sums = total[...]
    res[pl.ds(0, 4, stride=2), :] = sums
    res[pl.ds(1, 4, stride=2), :] = pltpu.roll(sums, 64, 1)
    pooled = res[:, :64]
    center = jnp.mean(pooled, axis=1, keepdims=True)
    spread = jnp.mean((pooled - center) ** 2, axis=1, keepdims=True)
    normed = ((pooled - center) / jnp.sqrt(spread + EPSILON) * gain[...]).astype(BF16)
    out[...] = jnp.dot(normed, wp[...], preferred_element_type=F32).astype(BF16)

    @pl.loop(0, 18)
    def _(k):
        @pl.when(lax.rem(me - c - 1 + k + n_all, n_all) != me)
        def _():
            pltpu.make_async_copy(rsend.at[k], rsend.at[k], row_send.at[k]).wait()

    @pl.loop(0, 10)
    def _(k):
        @pl.when(lax.rem(8 * c - 1 + k + n_all, n_all) != me)
        def _():
            pltpu.make_async_copy(csend.at[k], csend.at[k], col_send.at[k]).wait()


def body(pair, tile_mask, w_first, b_first, w_second, b_second, norm_gain, w_proj):
    n_row, n_col = lax.axis_size("row"), lax.axis_size("col")
    vmem = pl.BlockSpec(memory_space=pltpu.VMEM)
    return pl.pallas_call(
        functools.partial(kernel, n_row, n_col),
        out_shape=jax.ShapeDtypeStruct((8, w_proj.shape[1]), BF16),
        in_specs=[pl.BlockSpec(memory_space=pl.ANY), pl.BlockSpec(memory_space=pltpu.SMEM)] + [vmem] * 6,
        out_specs=vmem,
        scratch_shapes=[
            pltpu.VMEM((ROWS + 2 * EDGE, LANES + 256), BF16),
            pltpu.VMEM((ROWS, LANES + 256), BF16),
            pltpu.VMEM((ROWS, LANES + 256), BF16),
            pltpu.VMEM((ROWS, LANES), BF16),
            pltpu.VMEM((1536, 256), BF16),
            pltpu.VMEM((1152, 128), BF16),
            pltpu.VMEM((8, 256), F32),
            pltpu.VMEM((3, ROWS, 128), F32),
            pltpu.VMEM((ROWS, 128), F32),
            pltpu.VMEM((144, 128), F32),
            pltpu.VMEM((48, 128), F32),
            pltpu.VMEM((512, 128), F32),
            pltpu.VMEM((18, 4, 128), F32),
            pltpu.VMEM((10, 4, 128), F32),
            pltpu.VMEM((32, 4, 128), F32),
            pltpu.VMEM((16, 4, 128), F32),
            pltpu.VMEM((4, 128), F32),
            pltpu.VMEM((8, 128), F32),
            pltpu.SemaphoreType.DMA,
            pltpu.SemaphoreType.DMA((8,)),
            pltpu.SemaphoreType.DMA((8,)),
            pltpu.SemaphoreType.DMA((18,)),
            pltpu.SemaphoreType.DMA((32,)),
            pltpu.SemaphoreType.DMA((10,)),
            pltpu.SemaphoreType.DMA((16,)),
        ],
        compiler_params=pltpu.CompilerParams(
            collective_id=0, has_side_effects=True, vmem_limit_bytes=40 * 1024 * 1024
        ),
        name="block",
    )(
        pair, tile_mask, w_first, b_first.reshape(1, -1), w_second, b_second.reshape(1, -1),
        norm_gain.reshape(1, -1), w_proj,
    )


def solution(mesh):
    return jax.shard_map(
        body,
        mesh=mesh,
        in_specs=(P("row", "col"), P(), P(), P(), P(), P(), P(), P()),
        out_specs=P(("row", "col"), None),
        check_vma=False,
    )
```

time: 239 us -> 33.8 us (0.14)
  waiting for transfers between devices: 155 us -> 0 us
  Pallas kernels: 0 us -> 27.7 us
  starting transfers between devices: 25.5 us -> 0 us
  local copies, waits for them, and re-layouts: 21.6 us -> 5.81 us
  between operations: 13.8 us -> 0.02 us
  matrix products: 12.3 us -> 0 us
  other arithmetic: 10.7 us -> 0 us
    unnamed x2 -> x0, waiting for transfers between devices: 149 us -> none
    pallas_call x0 -> x1, Pallas kernels: none -> 27.7 us  [body(): pl.pallas_call(functools.partial(kernel, n_row, n_col), out_shape=jax.Sha...]
    ppermute x8 -> x0, starting transfers between devices: 25.5 us -> none  [the longest x4 18.9 us: with_halo(): lax.ppermute(tail, axis, [(i, (i + 1) % count) for i in range(ends)])]
    dot_general x19 -> x0, matrix products: 12.3 us -> none  [the longest x18 10.8 us: apply_taps(): jnp.einsum('rcx,xy->rcy', piece, kernel[tap_row, tap_col], preferred_elem...]
    scatter x4 -> x0, local copies, waits for them, and re-layouts: 8.28 us -> none  [the longest x2 8.18 us: packed_kernel(): return doubled.at[:, :, channels:, channels:].set(weight)]
    concatenate x4 -> x0, other arithmetic: 6.14 us -> none  [the longest x2 5.99 us: with_halo(): jnp.concatenate([lax.ppermute(tail, axis, [(i, (i + 1) % count) for i in...]
    ppermute x8 -> x0, waiting for transfers between devices: 5.43 us -> none  [the longest x4 5.42 us: with_halo(): lax.ppermute(head, axis, [((i + 1) % count, i) for i in range(ends)])]
    convert_element_type x2 -> x0, local copies, waits for them, and re-layouts: 3.51 us -> none  [the longest x1 1.87 us: body(): row_part = jnp.sum(cells, axis=1, dtype=jnp.float32)]
  transfers between devices with their start and end apart: 9 -> 0, of which waited for: 3 -> 0; matrix products, arithmetic and copies ran while one was open for 6% -> 0% of each run, Pallas kernels for 0% -> 0%
where the time goes in v1:
time: 33.8 us; the launch traced here: 33.5 us
  Pallas kernels  27.7 us (82%)
  local copies, waits for them, and re-layouts  5.81 us (17%)
    pallas_call x1, Pallas kernels, body(): pl.pallas_call(functools.partial(kernel, n_row, n_col), out_shape=jax.Sha...  27.7 us
    unnamed x17, local copies, waits for them, and re-layouts  5.81 us

profile of v1, /device:TPU:1, one launch (start us, length us, event | category | flops | bytes accessed | tf_op | source)
XLA Modules:
  0.0 33.5 jit_solution(8133328183898565327)
XLA Ops:
  0.0 0.0 copy-start.5
  0.0 0.0 copy-start.6
  0.0 0.0 copy-start.7
  0.0 0.6 %copy-done.5 = f32[64]{0:T(128)S(1)} copy-done((f32[64]{0:T(128)S(1)}, f32[64]{0:T(128)}, u32[]{:S(2)}) %copy-start.5) | copy-done | bytes 280
  0.7 0.0 copy-done.6
  0.7 0.0 copy-done.7
  0.7 0.0 copy-start
  0.7 1.2 %copy-done = bf16[128,4096]{1,0:T(8,128)(2,1)S(1)} copy-done((bf16[128,4096]{1,0:T(8,128)(2,1)S(1)}, bf16[128,4096]{1,0:T(8,128)(2,1)}, u32[]{:S(2)}) %copy-start) | copy-done | bytes 1048600
  1.9 0.0 copy-start.1
  1.9 0.9 %copy-done.1 = bf16[3,3,64,64]{3,2,1,0:T(8,128)(2,1)S(1)} copy-done((bf16[3,3,64,64]{3,2,1,0:T(8,128)(2,1)S(1)}, bf16[3,3,64,64]{3,2,1,0:T(8,128)(2,1)}, u32[]{:S(2)}) %copy-start.1) | copy-done | bytes 73752
  2.8 0.0 copy-start.2
  2.8 0.9 %copy-done.2 = bf16[3,3,64,64]{3,2,1,0:T(8,128)(2,1)S(1)} copy-done((bf16[3,3,64,64]{3,2,1,0:T(8,128)(2,1)S(1)}, bf16[3,3,64,64]{3,2,1,0:T(8,128)(2,1)}, u32[]{:S(2)}) %copy-start.2) | copy-done | bytes 73752
  3.7 0.0 copy-start.3
  3.7 0.8 %copy-done.3 = bf16[64,384]{1,0:T(8,128)(2,1)S(1)} copy-done((bf16[64,384]{1,0:T(8,128)(2,1)S(1)}, bf16[64,384]{1,0:T(8,128)(2,1)}, u32[]{:S(2)}) %copy-start.3) | copy-done | bytes 49176
  4.5 0.0 copy-start.4
  4.5 0.7 %copy-done.4 = s32[16,16]{1,0:T(8,128)S(1)} copy-done((s32[16,16]{1,0:T(8,128)S(1)}, s32[16,16]{1,0:T(8,128)}, u32[]{:S(2)}) %copy-start.4) | copy-done | bytes 1048
  5.2 27.7 %block.1 = bf16[8,384]{1,0:T(8,128)(2,1)S(1)} custom-call(bf16[128,4096]{1,0:T(8,128)(2,1)S(1)} %copy-done, s32[16,16]{1,0:T(8,128)S(1)} %copy-done.4, bf16[3,3,64,64]{3,2,1,0:T(8,128)(2,1)S(1)} %copy-done.1, f32[1,64]{1,0:T(1,128)S(1)} %bitcast.3, bf16[3,3,64,64]{3,2,1,0:T(8,128)(2,1)S(1)} %copy-done.2, f32[1,64]{1,0:T(1,128)S(1)} %bitcast.4, ...), custom_call_target="tpu_custom_call" | custom-call | tf_op jit(solution)/shard_map/block/pallas_call | solution.py:363
  32.9 0.6 %copy.10 = bf16[8,384]{1,0:T(8,128)(2,1)} copy(bf16[8,384]{1,0:T(8,128)(2,1)S(1)} %block.1) | data formatting | bytes 12288
Async XLA Ops:
  0.0 0.7 %copy-start.5 = (f32[64]{0:T(128)S(1)}, f32[64]{0:T(128)}, u32[]{:S(2)}) copy-start(f32[64]{0:T(128)} %param.11) | copy-start | bytes 772
  0.0 0.7 %copy-start.6 = (f32[64]{0:T(128)S(1)}, f32[64]{0:T(128)}, u32[]{:S(2)}) copy-start(f32[64]{0:T(128)} %param.13) | copy-start | bytes 772
  0.0 0.7 %copy-start.7 = (f32[64]{0:T(128)S(1)}, f32[64]{0:T(128)}, u32[]{:S(2)}) copy-start(f32[64]{0:T(128)} %param.14) | copy-start | bytes 772
  0.7 1.2 %copy-start = (bf16[128,4096]{1,0:T(8,128)(2,1)S(1)}, bf16[128,4096]{1,0:T(8,128)(2,1)}, u32[]{:S(2)}) copy-start(bf16[128,4096]{1,0:T(8,128)(2,1)} %pair.1) | copy-start | bytes 3145732
  1.9 0.9 %copy-start.1 = (bf16[3,3,64,64]{3,2,1,0:T(8,128)(2,1)S(1)}, bf16[3,3,64,64]{3,2,1,0:T(8,128)(2,1)}, u32[]{:S(2)}) copy-start(bf16[3,3,64,64]{3,2,1,0:T(8,128)(2,1)} %w1.1) | copy-start | bytes 221188
  2.8 0.9 %copy-start.2 = (bf16[3,3,64,64]{3,2,1,0:T(8,128)(2,1)S(1)}, bf16[3,3,64,64]{3,2,1,0:T(8,128)(2,1)}, u32[]{:S(2)}) copy-start(bf16[3,3,64,64]{3,2,1,0:T(8,128)(2,1)} %w2.1) | copy-start | bytes 221188
  3.7 0.8 %copy-start.3 = (bf16[64,384]{1,0:T(8,128)(2,1)S(1)}, bf16[64,384]{1,0:T(8,128)(2,1)}, u32[]{:S(2)}) copy-start(bf16[64,384]{1,0:T(8,128)(2,1)} %wp.1) | copy-start | bytes 147460
  4.5 0.7 %copy-start.4 = (s32[16,16]{1,0:T(8,128)S(1)}, s32[16,16]{1,0:T(8,128)}, u32[]{:S(2)}) copy-start(s32[16,16]{1,0:T(8,128)} %mask.1) | copy-start | bytes 3076

commit v2 on v1

--- a/solution.py
+++ b/solution.py
@@ -27,18 +27,30 @@
 
 def kernel(
     n_row, n_col,
-    pair, mask, w1, b1, w2, b2, gain, wp,
+    pair, mask_in, w1_in, b1_in, w2_in, b2_in, gain_in, wp_in,
     out,
-    xe, xm, xp, hb, wt1, wt2, bias, hs, xs, racc, cacc, csum, rsend, csend, rrecv, crecv, total, res,
-    load_sem, halo_send, halo_recv, row_send, row_recv, col_send, col_recv,
+    mask, w1, b1, w2, b2, gain, wp, xe, xm, xp, hb, wt1, wt2, hs, xs, racc, cacc, csum, packed, landed, rsend, csend, rrecv, crecv, total, res,
+    load_sem, small_sem, halo_send, halo_recv, row_send, row_recv, col_send, col_recv,
 ):
     r = lax.axis_index("row")
     c = lax.axis_index("col")
     me = r * n_col + c
     n_all = n_row * n_col
 
-    load = pltpu.make_async_copy(pair, xe.at[pl.ds(EDGE, ROWS), pl.ds(OWN, LANES)], load_sem)
-    load.start()
+    loads = [
+        pltpu.make_async_copy(
+            pair.at[pl.ds(start, size)], xe.at[pl.ds(EDGE + start, size), pl.ds(OWN, LANES)], load_sem.at[k]
+        )
+        for k, (start, size) in enumerate(((0, EDGE), (ROWS - EDGE, EDGE), (EDGE, ROWS - 2 * EDGE)))
+    ]
+    for copy in loads:
+        copy.start()
+    small = [(mask_in, mask), (w1_in, w1), (w2_in, w2), (b1_in, b1), (b2_in, b2), (gain_in, gain), (wp_in, wp)]
+    small = [
+        pltpu.make_async_copy(src, dst, small_sem.at[k]) for k, (src, dst) in enumerate(small)
+    ]
+    for copy in small:
+        copy.start()
 
     barrier = pltpu.get_barrier_semaphore()
 
@@ -54,17 +66,16 @@
     top, bottom = pl.ds(0, EDGE), pl.ds(ROWS - EDGE, EDGE)
     first, last = pl.ds(0, 128), pl.ds(LANES - 128, 128)
     above, below, whole = pl.ds(0, EDGE), pl.ds(EDGE + ROWS, EDGE), pl.ds(EDGE, ROWS)
-    before, after, inside = pl.ds(0, 128), pl.ds(OWN + LANES, 128), pl.ds(OWN, LANES)
-    every, every_row = pl.ds(0, LANES), pl.ds(0, ROWS)
+    before, after = pl.ds(0, 128), pl.ds(OWN + LANES, 128)
     halos = [
-        (up, c, top, every, below, inside),
-        (down, c, bottom, every, above, inside),
-        (r, left, every_row, first, whole, after),
-        (r, right, every_row, last, whole, before),
-        (up, left, top, first, below, after),
-        (up, right, top, last, below, before),
-        (down, left, bottom, first, above, after),
-        (down, right, bottom, last, above, before),
+        (up, c, packed.at[0], landed.at[1]),
+        (down, c, packed.at[1], landed.at[0]),
+        (r, left, pair.at[:, first], xe.at[whole, after]),
+        (r, right, pair.at[:, last], xe.at[whole, before]),
+        (up, left, pair.at[top, first], xe.at[below, after]),
+        (up, right, pair.at[top, last], xe.at[below, before]),
+        (down, left, pair.at[bottom, first], xe.at[above, after]),
+        (down, right, pair.at[bottom, last], xe.at[above, before]),
     ]
     for halo in halos:
         pl.semaphore_signal(barrier, inc=1, device_id=(halo[0], halo[1]), device_id_type=MESH)
@@ -95,6 +106,36 @@
             @pl.loop(0, n_row)
             def _(k):
                 greet(k, lax.rem(block + step, n_col))
+
+    to_self = lax.rem(me - 8 * c + 1 + n_all, n_all) < 10
+    pl.semaphore_wait(barrier, 8 + (n_col - 1) + 2 + 10 - jnp.where(to_self, 1, 0))
+    copies = []
+
+    def send(k):
+        tr, tc, src, dst = halos[k]
+        copy = pltpu.make_async_remote_copy(
+            src_ref=src, dst_ref=dst, send_sem=halo_send.at[k], recv_sem=halo_recv.at[k],
+            device_id=(tr, tc), device_id_type=MESH,
+        )
+        copy.start()
+        copies.append(copy)
+
+    for k in range(2, 8):
+        send(k)
+
+    for k, row in ((0, 0), (1, EDGE - 2)):
+        loads[k].wait()
+        cells = jnp.concatenate(
+            [xe[pl.ds(EDGE + (ROWS - EDGE) * k, EDGE), pl.ds(OWN + 512 * p, 512)] for p in range(8)], axis=0
+        )
+        i = lax.broadcasted_iota(jnp.int32, (16, 128), 0)
+        j = lax.broadcasted_iota(jnp.int32, (16, 128), 1)
+        select = jnp.where(j == (i // 2) * 16 + row + i % 2, 1.0, 0.0).astype(BF16)
+        packed[k] = jnp.dot(select, cells, preferred_element_type=F32).astype(BF16)
+        send(k)
+
+    for copy in small:
+        copy.wait()
 
     zero = jnp.zeros((64, 64), BF16)
     wt1[...] = jnp.zeros_like(wt1)
@@ -127,22 +168,7 @@
             rows < 0, mt[0][v], jnp.where(rows < 64, mt[1][v], jnp.where(rows < 128, mt[2][v], mt[3][v]))
         )
 
-    to_self = lax.rem(me - 8 * c + 1 + n_all, n_all) < 10
-    pl.semaphore_wait(barrier, 8 + (n_col - 1) + 2 + 10 - jnp.where(to_self, 1, 0))
-    copies = []
-    for k, (tr, tc, src_rows, src_lanes, dst_rows, dst_lanes) in enumerate(halos):
-        copy = pltpu.make_async_remote_copy(
-            src_ref=pair.at[src_rows, src_lanes],
-            dst_ref=xe.at[dst_rows, dst_lanes],
-            send_sem=halo_send.at[k],
-            recv_sem=halo_recv.at[k],
-            device_id=(tr, tc),
-            device_id_type=MESH,
-        )
-        copy.start()
-        copies.append(copy)
-
-    load.wait()
+    loads[2].wait()
 
     def shift(r0, lanes):
         window = xe[pl.ds(r0, 48), lanes]
@@ -183,6 +209,15 @@
 
     for copy in copies:
         copy.wait()
+
+    i = lax.broadcasted_iota(jnp.int32, (128, 16), 0)
+    j = lax.broadcasted_iota(jnp.int32, (128, 16), 1)
+    for k, (row, place) in enumerate(((EDGE - 2, above), (0, below))):
+        at_row = i % 16 - row
+        select = jnp.where((at_row >= 0) & (at_row < 2) & (j == (i // 16) * 2 + at_row), 1.0, 0.0)
+        cells = jnp.dot(select.astype(BF16), landed[k], preferred_element_type=F32).astype(BF16)
+        for p in range(8):
+            xe[place, pl.ds(OWN + 512 * p, 512)] = cells[16 * p : 16 * p + 16]
 
     @pl.when(r == 0)
     def _():
@@ -359,32 +394,41 @@
 
 def body(pair, tile_mask, w_first, b_first, w_second, b_second, norm_gain, w_proj):
     n_row, n_col = lax.axis_size("row"), lax.axis_size("col")
-    vmem = pl.BlockSpec(memory_space=pltpu.VMEM)
+    hbm = pl.BlockSpec(memory_space=pltpu.HBM)
     return pl.pallas_call(
         functools.partial(kernel, n_row, n_col),
         out_shape=jax.ShapeDtypeStruct((8, w_proj.shape[1]), BF16),
-        in_specs=[pl.BlockSpec(memory_space=pl.ANY), pl.BlockSpec(memory_space=pltpu.SMEM)] + [vmem] * 6,
-        out_specs=vmem,
+        in_specs=[hbm] * 8,
+        out_specs=pl.BlockSpec(memory_space=pltpu.VMEM),
         scratch_shapes=[
+            pltpu.SMEM(tile_mask.shape, jnp.int32),
+            pltpu.VMEM(w_first.shape, BF16),
+            pltpu.VMEM((1, 64), F32),
+            pltpu.VMEM(w_second.shape, BF16),
+            pltpu.VMEM((1, 64), F32),
+            pltpu.VMEM((1, 64), F32),
+            pltpu.VMEM(w_proj.shape, BF16),
             pltpu.VMEM((ROWS + 2 * EDGE, LANES + 256), BF16),
             pltpu.VMEM((ROWS, LANES + 256), BF16),
             pltpu.VMEM((ROWS, LANES + 256), BF16),
             pltpu.VMEM((ROWS, LANES), BF16),
             pltpu.VMEM((1536, 256), BF16),
             pltpu.VMEM((1152, 128), BF16),
-            pltpu.VMEM((8, 256), F32),
             pltpu.VMEM((3, ROWS, 128), F32),
             pltpu.VMEM((ROWS, 128), F32),
             pltpu.VMEM((144, 128), F32),
             pltpu.VMEM((48, 128), F32),
             pltpu.VMEM((512, 128), F32),
+            pltpu.VMEM((2, 16, 512), BF16),
+            pltpu.VMEM((2, 16, 512), BF16),
             pltpu.VMEM((18, 4, 128), F32),
             pltpu.VMEM((10, 4, 128), F32),
             pltpu.VMEM((32, 4, 128), F32),
             pltpu.VMEM((16, 4, 128), F32),
             pltpu.VMEM((4, 128), F32),
             pltpu.VMEM((8, 128), F32),
-            pltpu.SemaphoreType.DMA,
+            pltpu.SemaphoreType.DMA((3,)),
+            pltpu.SemaphoreType.DMA((7,)),
             pltpu.SemaphoreType.DMA((8,)),
             pltpu.SemaphoreType.DMA((8,)),
             pltpu.SemaphoreType.DMA((18,)),
@@ -393,7 +437,7 @@
             pltpu.SemaphoreType.DMA((16,)),
         ],
         compiler_params=pltpu.CompilerParams(
-            collective_id=0, has_side_effects=True, vmem_limit_bytes=40 * 1024 * 1024
+            collective_id=0, has_side_effects=True, vmem_limit_bytes=64 * 1024 * 1024 - 65536
         ),
         name="block",
     )(

time: 33.8 us -> 25.9 us (0.77)
  local copies, waits for them, and re-layouts: 5.81 us -> 1.29 us
  Pallas kernels: 27.7 us -> 24.5 us
    unnamed x17 -> x1, local copies, waits for them, and re-layouts: 5.81 us -> 1.29 us
    pallas_call x1, Pallas kernels: 27.7 us -> 24.5 us  [body(): pl.pallas_call(functools.partial(kernel, n_row, n_col), out_shape=jax.Sha...]
where the time goes in v2:
time: 25.9 us; the launch traced here: 25.8 us
  Pallas kernels  24.5 us (95%)
  local copies, waits for them, and re-layouts  1.29 us (5%)
    pallas_call x1, Pallas kernels, body(): pl.pallas_call(functools.partial(kernel, n_row, n_col), out_shape=jax.Sha...  24.5 us
    unnamed x1, local copies, waits for them, and re-layouts  1.29 us

profile of v2, /device:TPU:1, one launch (start us, length us, event | category | flops | bytes accessed | tf_op | source)
XLA Modules:
  0.0 25.8 jit_solution(17722144140627929909)
XLA Ops:
  0.0 24.5 %block.1 = bf16[8,384]{1,0:T(8,128)(2,1)} custom-call(bf16[128,4096]{1,0:T(8,128)(2,1)} %pair.1, s32[16,16]{1,0:T(8,128)} %mask_in.1, bf16[3,3,64,64]{3,2,1,0:T(8,128)(2,1)} %w1_in.1, f32[1,64]{1,0:T(1,128)} %bitcast.3, bf16[3,3,64,64]{3,2,1,0:T(8,128)(2,1)} %w2_in.1, f32[1,64]{1,0:T(1,128)} %bitcast.4, f32[1,64]{1,0:T(1,128)} %bitcast.5, bf16[64,384]{1,0:T(8,128)(2,1)} %wp_in.1), custom_call_target="tpu_custom_call" | custom-call | tf_op jit(solution)/shard_map/block/pallas_call | solution.py:398
  24.5 1.3 %copy.10 = bf16[8,384]{1,0:T(8,128)(2,1)} copy(bf16[8,384]{1,0:T(8,128)(2,1)} %block.1) | data formatting | bytes 12288

commit v3 on v2

--- a/solution.py
+++ b/solution.py
@@ -30,7 +30,7 @@
     pair, mask_in, w1_in, b1_in, w2_in, b2_in, gain_in, wp_in,
     out,
     mask, w1, b1, w2, b2, gain, wp, xe, xm, xp, hb, wt1, wt2, hs, xs, racc, cacc, csum, packed, landed, rsend, csend, rrecv, crecv, total, res,
-    load_sem, small_sem, halo_send, halo_recv, row_send, row_recv, col_send, col_recv,
+    ready, load_sem, small_sem, halo_send, halo_recv, row_send, row_recv, col_send, col_recv,
 ):
     r = lax.axis_index("row")
     c = lax.axis_index("col")
@@ -43,23 +43,14 @@
         )
         for k, (start, size) in enumerate(((0, EDGE), (ROWS - EDGE, EDGE), (EDGE, ROWS - 2 * EDGE)))
     ]
-    for copy in loads:
-        copy.start()
     small = [(mask_in, mask), (w1_in, w1), (w2_in, w2), (b1_in, b1), (b2_in, b2), (gain_in, gain), (wp_in, wp)]
     small = [
         pltpu.make_async_copy(src, dst, small_sem.at[k]) for k, (src, dst) in enumerate(small)
     ]
-    for copy in small:
-        copy.start()
-
     barrier = pltpu.get_barrier_semaphore()
 
-    def greet(tr, tc):
-        same = jnp.logical_and(tr == r, tc == c)
-
-        @pl.when(jnp.logical_not(same))
-        def _():
-            pl.semaphore_signal(barrier, inc=1, device_id=(tr, tc), device_id_type=MESH)
+    def greet(semaphore, tr, tc):
+        pl.semaphore_signal(semaphore, inc=1, device_id=(tr, tc), device_id_type=MESH)
 
     up, down = lax.rem(r + n_row - 1, n_row), lax.rem(r + 1, n_row)
     left, right = lax.rem(c + n_col - 1, n_col), lax.rem(c + 1, n_col)
@@ -77,41 +68,29 @@
         (down, left, pair.at[bottom, first], xe.at[above, after]),
         (down, right, pair.at[bottom, last], xe.at[above, before]),
     ]
-    for halo in halos:
-        pl.semaphore_signal(barrier, inc=1, device_id=(halo[0], halo[1]), device_id_type=MESH)
-
-    @pl.loop(1, n_col)
-    def _(k):
-        pl.semaphore_signal(
-            barrier, inc=1, device_id=(r, lax.rem(c + k, n_col)), device_id_type=MESH
-        )
-
-    for edge, other in ((0, up), (n_col - 1, down)):
-        @pl.when(c == edge)
-        def _():
-            @pl.loop(0, n_col)
-            def _(k):
-                pl.semaphore_signal(barrier, inc=1, device_id=(other, k), device_id_type=MESH)
-
-    block = me // 8
+    for k in range(1, n_row):
+        greet(barrier, lax.rem(r + k, n_row), c)
+    for halo in halos[4:]:
+        greet(barrier, halo[0], halo[1])
+    for k in range(1, n_col):
+        greet(barrier, r, lax.rem(c + k, n_col))
+    for copy in loads + small:
+        copy.start()
     part = lax.rem(me, 8)
 
-    @pl.loop(0, n_row)
-    def _(k):
-        greet(k, block)
-
-    for edge, step in ((0, n_col - 1), (7, 1)):
-        @pl.when(part == edge)
-        def _():
-            @pl.loop(0, n_row)
-            def _(k):
-                greet(k, lax.rem(block + step, n_col))
-
-    to_self = lax.rem(me - 8 * c + 1 + n_all, n_all) < 10
-    pl.semaphore_wait(barrier, 8 + (n_col - 1) + 2 + 10 - jnp.where(to_self, 1, 0))
+    for k, row in ((0, 0), (1, EDGE - 2)):
+        loads[k].wait()
+        cells = jnp.concatenate(
+            [xe[pl.ds(EDGE + (ROWS - EDGE) * k, EDGE), pl.ds(OWN + 512 * p, 512)] for p in range(8)], axis=0
+        )
+        i = lax.broadcasted_iota(jnp.int32, (16, 128), 0)
+        j = lax.broadcasted_iota(jnp.int32, (16, 128), 1)
+        select = jnp.where(j == (i // 2) * 16 + row + i % 2, 1.0, 0.0).astype(BF16)
+        packed[k] = jnp.dot(select, cells, preferred_element_type=F32).astype(BF16)
+
+    pl.semaphore_wait(barrier, (n_row - 1) + 4 + (n_col - 1))
     copies = []
-
-    def send(k):
+    for k in (0, 1, 4, 5, 6, 7, 2, 3):
         tr, tc, src, dst = halos[k]
         copy = pltpu.make_async_remote_copy(
             src_ref=src, dst_ref=dst, send_sem=halo_send.at[k], recv_sem=halo_recv.at[k],
@@ -119,20 +98,8 @@
         )
         copy.start()
         copies.append(copy)
-
-    for k in range(2, 8):
-        send(k)
-
-    for k, row in ((0, 0), (1, EDGE - 2)):
-        loads[k].wait()
-        cells = jnp.concatenate(
-            [xe[pl.ds(EDGE + (ROWS - EDGE) * k, EDGE), pl.ds(OWN + 512 * p, 512)] for p in range(8)], axis=0
-        )
-        i = lax.broadcasted_iota(jnp.int32, (16, 128), 0)
-        j = lax.broadcasted_iota(jnp.int32, (16, 128), 1)
-        select = jnp.where(j == (i // 2) * 16 + row + i % 2, 1.0, 0.0).astype(BF16)
-        packed[k] = jnp.dot(select, cells, preferred_element_type=F32).astype(BF16)
-        send(k)
+    for k in range(1, n_col):
+        greet(ready, r, lax.rem(c + k, n_col))
 
     for copy in small:
         copy.wait()
@@ -207,6 +174,21 @@
         hs[1, pl.ds(r0, 16), :] = fold(hidden(r0, 16, range(1, GROUPS - 1)))
         sum_x(r0)
 
+    at = lax.broadcasted_iota(jnp.int32, (16, 128), 1)
+    own_at = by_row(at, 0)
+    for g in range(GROUPS):
+        sums = jnp.dot(
+            own_at.astype(BF16), xe[pl.ds(EDGE, ROWS), pl.ds(OWN + g * 256, 256)], preferred_element_type=F32
+        )
+        csum[pl.ds(g * 32, 16), :] = sums[:, :128]
+        csum[pl.ds(g * 32 + 16, 16), :] = sums[:, 128:]
+    cacc[...] = jnp.zeros_like(cacc)
+    cacc[pl.ds(8, PAIRS), :] = csum[pl.ds(0, PAIRS, stride=16), :] + bias_two * (
+        64.0 * (mt[1][0] + mt[2][0])
+    )
+    sum_x(0)
+    sum_x(ROWS - 16)
+
     for copy in copies:
         copy.wait()
 
@@ -247,7 +229,6 @@
         hs[0, pl.ds(r0, 16), :] = fold(parts[:1])
         hs[1, pl.ds(r0, 16), :] = fold(parts[1:-1])
         hs[2, pl.ds(r0, 16), :] = fold(parts[-1:])
-        sum_x(r0)
 
     parts = hidden(16, ROWS - 32, (0, GROUPS - 1))
     hs[0, pl.ds(16, ROWS - 32), :] = fold(parts[:1])
@@ -256,6 +237,56 @@
     def split(values):
         high = values.astype(BF16)
         return jnp.concatenate([high, (values - high.astype(F32)).astype(BF16)], axis=0)
+
+    combos = [(a, v) for a in range(3) for v in range(3)]
+    which = lax.broadcasted_iota(jnp.int32, (16, 128), 0)
+    pick = jnp.zeros((16, 128), F32)
+    for k, (a, v) in enumerate(combos):
+        pick = jnp.where(which == k, by_row(at - 4 * (a - 1), v), pick)
+    pick = (pick * own_at).astype(BF16)
+    for g in range(GROUPS):
+        sums = jnp.dot(pick, hb[:, pl.ds(g * 256, 256)], preferred_element_type=F32)
+        csum[pl.ds(g * 32, 16), :] = sums[:, :128]
+        csum[pl.ds(g * 32 + 16, 16), :] = sums[:, 128:]
+
+    def column(k):
+        return csum[pl.ds(k, PAIRS, stride=16), :]
+
+    at_pair = lax.broadcasted_iota(jnp.int32, (PAIRS, 128), 0)
+    for b in range(3):
+        pieces = []
+        for a in range(3):
+            value = column(3 * a)
+            if b == 0:
+                value = jnp.where(at_pair >= PAIRS - 2, column(3 * a + 2), value)
+            if b == 2:
+                value = jnp.where(at_pair < 2, column(3 * a + 1), value)
+            pieces.append(value)
+        weights = jnp.concatenate([wt2[pl.ds((a * 3 + b) * 128, 128), :] for a in range(3)], axis=0)
+        both = jnp.dot(split(jnp.concatenate(pieces, axis=1)), weights, preferred_element_type=F32)
+        cacc[pl.ds(8 - 2 * (b - 1), PAIRS), :] += both[:PAIRS] + both[PAIRS:]
+    columns = cacc[pl.ds(4, 40), :]
+    for k in range(10):
+        csend[k] = columns[4 * k : 4 * k + 4]
+
+    pl.semaphore_wait(ready, n_col - 1)
+
+    @pl.loop(0, 10)
+    def _(k):
+        target = lax.rem(8 * c - 1 + k + n_all, n_all)
+        slot = jnp.where((k == 0) | (k == 9), n_row + r, r)
+
+        @pl.when(target == me)
+        def _():
+            pltpu.make_async_copy(csend.at[k], crecv.at[slot], col_recv.at[slot]).start()
+
+        @pl.when(target != me)
+        def _():
+            pltpu.make_async_remote_copy(
+                src_ref=csend.at[k], dst_ref=crecv.at[slot], send_sem=col_send.at[k],
+                recv_sem=col_recv.at[slot], device_id=(target // n_col, lax.rem(target, n_col)),
+                device_id_type=MESH,
+            ).start()
 
     rows = lax.broadcasted_iota(jnp.int32, (ROWS, 128), 0)
     own = by_row(rows, 0)
@@ -297,61 +328,6 @@
             pltpu.make_async_remote_copy(
                 src_ref=rsend.at[k], dst_ref=rrecv.at[slot], send_sem=row_send.at[k],
                 recv_sem=row_recv.at[slot], device_id=(target // n_col, lax.rem(target, n_col)),
-                device_id_type=MESH,
-            ).start()
-
-    combos = [(a, v) for a in range(3) for v in range(3)]
-    at = lax.broadcasted_iota(jnp.int32, (16, 128), 1)
-    which = lax.broadcasted_iota(jnp.int32, (16, 128), 0)
-    own_at = by_row(at, 0)
-    pick = jnp.zeros((16, 128), F32)
-    for k, (a, v) in enumerate(combos):
-        pick = jnp.where(which == k, by_row(at - 4 * (a - 1), v), pick)
-    pick = jnp.concatenate([pick * own_at, jnp.where(which == 9, own_at, 0.0)], axis=1).astype(BF16)
-    for g in range(GROUPS):
-        cells = jnp.concatenate(
-            [hb[:, pl.ds(g * 256, 256)], xe[pl.ds(EDGE, ROWS), pl.ds(OWN + g * 256, 256)]], axis=0
-        )
-        sums = jnp.dot(pick, cells, preferred_element_type=F32)
-        csum[pl.ds(g * 32, 16), :] = sums[:, :128]
-        csum[pl.ds(g * 32 + 16, 16), :] = sums[:, 128:]
-
-    def column(k):
-        return csum[pl.ds(k, PAIRS, stride=16), :]
-
-    at_pair = lax.broadcasted_iota(jnp.int32, (PAIRS, 128), 0)
-    cacc[...] = jnp.zeros_like(cacc)
-    cacc[pl.ds(8, PAIRS), :] = column(9) + bias_two * (64.0 * (mt[1][0] + mt[2][0]))
-    for b in range(3):
-        pieces = []
-        for a in range(3):
-            value = column(3 * a)
-            if b == 0:
-                value = jnp.where(at_pair >= PAIRS - 2, column(3 * a + 2), value)
-            if b == 2:
-                value = jnp.where(at_pair < 2, column(3 * a + 1), value)
-            pieces.append(value)
-        weights = jnp.concatenate([wt2[pl.ds((a * 3 + b) * 128, 128), :] for a in range(3)], axis=0)
-        both = jnp.dot(split(jnp.concatenate(pieces, axis=1)), weights, preferred_element_type=F32)
-        cacc[pl.ds(8 - 2 * (b - 1), PAIRS), :] += both[:PAIRS] + both[PAIRS:]
-    columns = cacc[pl.ds(4, 40), :]
-    for k in range(10):
-        csend[k] = columns[4 * k : 4 * k + 4]
-
-    @pl.loop(0, 10)
-    def _(k):
-        target = lax.rem(8 * c - 1 + k + n_all, n_all)
-        slot = jnp.where((k == 0) | (k == 9), n_row + r, r)
-
-        @pl.when(target == me)
-        def _():
-            pltpu.make_async_copy(csend.at[k], crecv.at[slot], col_recv.at[slot]).start()
-
-        @pl.when(target != me)
-        def _():
-            pltpu.make_async_remote_copy(
-                src_ref=csend.at[k], dst_ref=crecv.at[slot], send_sem=col_send.at[k],
-                recv_sem=col_recv.at[slot], device_id=(target // n_col, lax.rem(target, n_col)),
                 device_id_type=MESH,
             ).start()
 
@@ -427,6 +403,7 @@
             pltpu.VMEM((16, 4, 128), F32),
             pltpu.VMEM((4, 128), F32),
             pltpu.VMEM((8, 128), F32),
+            pltpu.SemaphoreType.REGULAR,
             pltpu.SemaphoreType.DMA((3,)),
             pltpu.SemaphoreType.DMA((7,)),
             pltpu.SemaphoreType.DMA((8,)),

time: 25.9 us -> 25.1 us (0.969)
  the two profiles are of different devices: /device:TPU:1 before, /device:TPU:0 now
where the time goes in v3:
time: 25.1 us; the launch traced here: 24.9 us
  Pallas kernels  23.6 us (94%)
  local copies, waits for them, and re-layouts  1.29 us (5%)
    pallas_call x1, Pallas kernels, body(): pl.pallas_call(functools.partial(kernel, n_row, n_col), out_shape=jax.Sha...  23.6 us
    unnamed x1, local copies, waits for them, and re-layouts  1.29 us

profile of v3, /device:TPU:0, one launch (start us, length us, event | category | flops | bytes accessed | tf_op | source)
XLA Modules:
  0.0 24.9 jit_solution(12341504383553427194)
XLA Ops:
  0.0 23.6 %block.1 = bf16[8,384]{1,0:T(8,128)(2,1)} custom-call(bf16[128,4096]{1,0:T(8,128)(2,1)} %pair.1, s32[16,16]{1,0:T(8,128)} %mask_in.1, bf16[3,3,64,64]{3,2,1,0:T(8,128)(2,1)} %w1_in.1, f32[1,64]{1,0:T(1,128)} %bitcast.3, bf16[3,3,64,64]{3,2,1,0:T(8,128)(2,1)} %w2_in.1, f32[1,64]{1,0:T(1,128)} %bitcast.4, f32[1,64]{1,0:T(1,128)} %bitcast.5, bf16[64,384]{1,0:T(8,128)(2,1)} %wp_in.1), custom_call_target="tpu_custom_call" | custom-call | tf_op jit(solution)/shard_map/block/pallas_call | solution.py:374
  23.6 1.3 %copy.10 = bf16[8,384]{1,0:T(8,128)(2,1)} copy(bf16[8,384]{1,0:T(8,128)(2,1)} %block.1) | data formatting | bytes 12288

commit v4 on v3

--- a/solution.py
+++ b/solution.py
@@ -54,19 +54,19 @@
 
     up, down = lax.rem(r + n_row - 1, n_row), lax.rem(r + 1, n_row)
     left, right = lax.rem(c + n_col - 1, n_col), lax.rem(c + 1, n_col)
-    top, bottom = pl.ds(0, EDGE), pl.ds(ROWS - EDGE, EDGE)
-    first, last = pl.ds(0, 128), pl.ds(LANES - 128, 128)
     above, below, whole = pl.ds(0, EDGE), pl.ds(EDGE + ROWS, EDGE), pl.ds(EDGE, ROWS)
     before, after = pl.ds(0, 128), pl.ds(OWN + LANES, 128)
+    first, last = pl.ds(OWN, 128), pl.ds(OWN + LANES - 128, 128)
+    top, bottom = pl.ds(EDGE, EDGE), pl.ds(ROWS, EDGE)
     halos = [
         (up, c, packed.at[0], landed.at[1]),
         (down, c, packed.at[1], landed.at[0]),
-        (r, left, pair.at[:, first], xe.at[whole, after]),
-        (r, right, pair.at[:, last], xe.at[whole, before]),
-        (up, left, pair.at[top, first], xe.at[below, after]),
-        (up, right, pair.at[top, last], xe.at[below, before]),
-        (down, left, pair.at[bottom, first], xe.at[above, after]),
-        (down, right, pair.at[bottom, last], xe.at[above, before]),
+        (r, left, xe.at[whole, first], xe.at[whole, after]),
+        (r, right, xe.at[whole, last], xe.at[whole, before]),
+        (up, left, xe.at[top, first], xe.at[below, after]),
+        (up, right, xe.at[top, last], xe.at[below, before]),
+        (down, left, xe.at[bottom, first], xe.at[above, after]),
+        (down, right, xe.at[bottom, last], xe.at[above, before]),
     ]
     for k in range(1, n_row):
         greet(barrier, lax.rem(r + k, n_row), c)
@@ -88,6 +88,7 @@
         select = jnp.where(j == (i // 2) * 16 + row + i % 2, 1.0, 0.0).astype(BF16)
         packed[k] = jnp.dot(select, cells, preferred_element_type=F32).astype(BF16)
 
+    loads[2].wait()
     pl.semaphore_wait(barrier, (n_row - 1) + 4 + (n_col - 1))
     copies = []
     for k in (0, 1, 4, 5, 6, 7, 2, 3):
@@ -134,8 +135,6 @@
         return jnp.where(
             rows < 0, mt[0][v], jnp.where(rows < 64, mt[1][v], jnp.where(rows < 128, mt[2][v], mt[3][v]))
         )
-
-    loads[2].wait()
 
     def shift(r0, lanes):
         window = xe[pl.ds(r0, 48), lanes]
@@ -373,7 +372,7 @@
     hbm = pl.BlockSpec(memory_space=pltpu.HBM)
     return pl.pallas_call(
         functools.partial(kernel, n_row, n_col),
-        out_shape=jax.ShapeDtypeStruct((8, w_proj.shape[1]), BF16),
+        out_shape=pltpu.VMEM((8, w_proj.shape[1]), BF16),
         in_specs=[hbm] * 8,
         out_specs=pl.BlockSpec(memory_space=pltpu.VMEM),
         scratch_shapes=[
@@ -414,13 +413,14 @@
             pltpu.SemaphoreType.DMA((16,)),
         ],
         compiler_params=pltpu.CompilerParams(
-            collective_id=0, has_side_effects=True, vmem_limit_bytes=64 * 1024 * 1024 - 65536
+            collective_id=0, has_side_effects=True, vmem_limit_bytes=48 * 1024 * 1024
         ),
         name="block",
     )(
+        *(pltpu.with_memory_space_constraint(v, pltpu.HBM) for v in (
         pair, tile_mask, w_first, b_first.reshape(1, -1), w_second, b_second.reshape(1, -1),
         norm_gain.reshape(1, -1), w_proj,
-    )
+    )))
 
 
 def solution(mesh):

time: 25.1 us -> 23.8 us (0.948)
  local copies, waits for them, and re-layouts: 1.29 us -> 0.6 us
  Pallas kernels: 23.6 us -> 23 us
    unnamed x1, local copies, waits for them, and re-layouts: 1.29 us -> 0.6 us
    pallas_call x1, Pallas kernels: 23.6 us -> 23 us  [body(): pl.pallas_call(functools.partial(kernel, n_row, n_col), out_shape=pltpu.V...]
where the time goes in v4:
time: 23.8 us; the launch traced here: 23.6 us
  Pallas kernels  23 us (97%)
  local copies, waits for them, and re-layouts  0.6 us (3%)
    pallas_call x1, Pallas kernels, body(): pl.pallas_call(functools.partial(kernel, n_row, n_col), out_shape=pltpu.V...  23 us
    unnamed x1, local copies, waits for them, and re-layouts  0.6 us

profile of v4, /device:TPU:0, one launch (start us, length us, event | category | flops | bytes accessed | tf_op | source)
XLA Modules:
  0.0 23.6 jit_solution(11464691467688797078)
XLA Ops:
  0.0 23.0 %block.1 = bf16[8,384]{1,0:T(8,128)(2,1)S(1)} custom-call(bf16[128,4096]{1,0:T(8,128)(2,1)} %pair.1, s32[16,16]{1,0:T(8,128)} %mask_in.1, bf16[3,3,64,64]{3,2,1,0:T(8,128)(2,1)} %w1_in.1, f32[1,64]{1,0:T(1,128)} %bitcast.3, bf16[3,3,64,64]{3,2,1,0:T(8,128)(2,1)} %w2_in.1, f32[1,64]{1,0:T(1,128)} %bitcast.4, f32[1,64]{1,0:T(1,128)} %bitcast.5, ...), custom_call_target="tpu_custom_call" | custom-call | tf_op jit(solution)/shard_map/block/pallas_call | solution.py:373
  23.0 0.6 %copy.10 = bf16[8,384]{1,0:T(8,128)(2,1)} copy(bf16[8,384]{1,0:T(8,128)(2,1)S(1)} %block.1) | data formatting | bytes 12288

commit v5 on v4

v5 whole, which is shorter than its diff:
```python
import functools

import jax
import jax.numpy as jnp
from jax import lax
from jax.experimental import pallas as pl
from jax.experimental.pallas import tpu as pltpu
from jax.sharding import PartitionSpec as P

TILE = 64
EPSILON = 1e-05
MESH = pl.DeviceIdType.MESH
F32 = jnp.float32
BF16 = jnp.bfloat16

ROWS = 128
PAIRS = 32
EDGE = 16
GROUPS = 16
OWN = 128
LANES = PAIRS * 128


def elu(v):
    return jnp.where(v > 0, v, jnp.exp(jnp.minimum(v, 0.0)) - 1.0)


def kernel(
    n_row, n_col,
    pair, mask_in, w1_in, b1_in, w2_in, b2_in, gain_in, wp_in,
    out,
    mask, w1, b1, w2, b2, gain, wp, xe, xm, xp, hb, wt1, wt2, hs, xs, racc, cacc, csum, compact, landed, side, side_pre, edge_pre, gather, rsend, csend, rrecv, crecv, res,
    ready, load_sem, small_sem, halo_send, halo_recv, row_send, row_recv, col_send, col_recv,
):
    r = lax.axis_index("row")
    c = lax.axis_index("col")
    me = r * n_col + c
    n_all = n_row * n_col

    loads = [
        pltpu.make_async_copy(
            pair.at[pl.ds(start, size)], xe.at[pl.ds(EDGE + start, size), pl.ds(OWN, LANES)], load_sem.at[k]
        )
        for k, (start, size) in enumerate(((0, EDGE), (ROWS - EDGE, EDGE), (EDGE, ROWS - 2 * EDGE)))
    ]
    small = [(mask_in, mask), (w1_in, w1), (w2_in, w2), (b1_in, b1), (b2_in, b2), (gain_in, gain), (wp_in, wp)]
    small = [
        pltpu.make_async_copy(src, dst, small_sem.at[k]) for k, (src, dst) in enumerate(small)
    ]
    barrier = pltpu.get_barrier_semaphore()

    def greet(semaphore, tr, tc):
        pl.semaphore_signal(semaphore, inc=1, device_id=(tr, tc), device_id_type=MESH)

    up, down = lax.rem(r + n_row - 1, n_row), lax.rem(r + 1, n_row)
    left, right = lax.rem(c + n_col - 1, n_col), lax.rem(c + 1, n_col)
    above, below, whole = pl.ds(0, EDGE), pl.ds(EDGE + ROWS, EDGE), pl.ds(EDGE, ROWS)
    before, after = pl.ds(0, 128), pl.ds(OWN + LANES, 128)
    first, last = pl.ds(OWN, 128), pl.ds(OWN + LANES - 128, 128)
    top, bottom = pl.ds(EDGE, EDGE), pl.ds(ROWS, EDGE)
    inner, low, high = pl.ds(EDGE, ROWS), pl.ds(0, EDGE), pl.ds(EDGE + ROWS, EDGE)
    halos = [
        (up, c, compact.at[0, pl.ds(16, 32)], landed.at[1, pl.ds(16, 32)]),
        (down, c, compact.at[3, pl.ds(16, 32)], landed.at[0, pl.ds(16, 32)]),
        (r, left, xe.at[whole, first], side.at[1, inner]),
        (r, right, xe.at[whole, last], side.at[0, inner]),
        (up, left, xe.at[top, first], side.at[1, high]),
        (up, right, xe.at[top, last], side.at[0, high]),
        (down, left, xe.at[bottom, first], side.at[1, low]),
        (down, right, xe.at[bottom, last], side.at[0, low]),
    ]
    for k in range(1, n_row):
        greet(barrier, lax.rem(r + k, n_row), c)
    for halo in halos[4:]:
        greet(barrier, halo[0], halo[1])
    for k in range(1, n_col):
        greet(barrier, r, lax.rem(c + k, n_col))
    for copy in loads + small:
        copy.start()
    part = lax.rem(me, 8)

    xe[above, :] = jnp.zeros((EDGE, xe.shape[1]), BF16)
    xe[below, :] = jnp.zeros((EDGE, xe.shape[1]), BF16)
    xe[whole, before] = jnp.zeros((ROWS, 128), BF16)
    xe[whole, after] = jnp.zeros((ROWS, 128), BF16)
    for k in range(2):
        landed[k, pl.ds(0, 16), :] = jnp.zeros((16, 256), BF16)
        landed[k, pl.ds(48, 16), :] = jnp.zeros((16, 256), BF16)
    for k in range(4):
        compact[k, pl.ds(0, 16), :] = jnp.zeros((16, 256), BF16)
        compact[k, pl.ds(48, 16), :] = jnp.zeros((16, 256), BF16)

    row_edge = (c == 0) | (c == n_col - 1)
    col_edge = (part == 0) | (part == 7)

    @pl.when(jnp.logical_not(row_edge))
    def _():
        rrecv[pl.ds(n_col, n_col)] = jnp.zeros((n_col, 4, 128), F32)

    @pl.when(jnp.logical_not(col_edge))
    def _():
        crecv[pl.ds(n_row, n_row)] = jnp.zeros((n_row, 4, 128), F32)

    i = lax.broadcasted_iota(jnp.int32, (64, 256), 0)
    j = lax.broadcasted_iota(jnp.int32, (64, 256), 1)
    for k in range(2):
        loads[k].wait()
        cells = jnp.concatenate(
            [xe[pl.ds(EDGE + (ROWS - EDGE) * k, EDGE), pl.ds(OWN + 256 * g, 256)] for g in range(GROUPS)], axis=0
        )
        row = (EDGE - 4) * k + (i // 32) * 2 + i % 2
        select = jnp.where(j == (i % 32 // 2) * 16 + row, 1.0, 0.0).astype(BF16)
        both = jnp.dot(select, cells, preferred_element_type=F32).astype(BF16)
        compact[2 * k, pl.ds(16, 32), :] = both[:32]
        compact[2 * k + 1, pl.ds(16, 32), :] = both[32:]

    loads[2].wait()
    pl.semaphore_wait(barrier, (n_row - 1) + 4 + (n_col - 1))
    copies = []
    for k in (0, 1, 4, 5, 6, 7, 2, 3):
        tr, tc, src, dst = halos[k]
        copy = pltpu.make_async_remote_copy(
            src_ref=src, dst_ref=dst, send_sem=halo_send.at[k], recv_sem=halo_recv.at[k],
            device_id=(tr, tc), device_id_type=MESH,
        )
        copy.start()
        copies.append(copy)
    for k in range(1, n_col):
        greet(ready, r, lax.rem(c + k, n_col))

    for copy in small:
        copy.wait()

    zero = jnp.zeros((64, 64), BF16)
    wt1[...] = jnp.zeros_like(wt1)
    for a in range(3):
        for b in range(3):
            w = w1[a, b]
            doubled = jnp.concatenate(
                [jnp.concatenate([w, zero], axis=1), jnp.concatenate([zero, w], axis=1)], axis=0
            )
            for n in range(2):
                wt1[pl.ds(a * 512 + (b + n) * 128, 128), pl.ds(n * 128, 128)] = doubled
            w = w2[a, b]
            wt2[pl.ds((a * 3 + b) * 128, 128), :] = jnp.concatenate(
                [jnp.concatenate([w, zero], axis=1), jnp.concatenate([zero, w], axis=1)], axis=0
            )
    bias_one = jnp.concatenate([b1[...]] * 4, axis=1)
    bias_two = jnp.concatenate([b2[...]] * 2, axis=1)

    def tile(t, v):
        ti = 2 * r - 1 + t
        tj = c + v
        ok = (ti >= 0) & (ti < 2 * n_row) & (tj >= 0) & (tj < n_col)
        value = mask[jnp.clip(ti, 0, 2 * n_row - 1), jnp.clip(tj, 0, n_col - 1)]
        return jnp.where(ok, value, 0).astype(F32)

    mt = [[tile(t, v) for v in (0, -1, 1)] for t in range(4)]

    def by_row(rows, v):
        return jnp.where(
            rows < 0, mt[0][v], jnp.where(rows < 64, mt[1][v], jnp.where(rows < 128, mt[2][v], mt[3][v]))
        )

    def expand(buffer, k):
        window = buffer[k]
        return jnp.concatenate([window[14:46, 128:], window[16:48], window[18:50, :128]], axis=1)

    def fold(parts):
        both = functools.reduce(jnp.add, parts)
        return both[:, :128] + both[:, 128:]

    def split(values):
        high_part = values.astype(BF16)
        return jnp.concatenate([high_part, (values - high_part.astype(F32)).astype(BF16)], axis=0)

    @pl.loop(0, ROWS // 16)
    def _(k):
        r0 = pl.multiple_of(16 * k, 16)
        window = xe[pl.ds(r0, 48), :]
        xm[...] = window[14:30]
        xp[...] = window[18:34]
        lhs = []
        for g in range(GROUPS):
            lanes = pl.ds(g * 256, 512)
            lhs.append(jnp.concatenate([xm[:, lanes], xe[pl.ds(EDGE + r0, 16), lanes], xp[:, lanes]], axis=1))
        pre = jnp.dot(jnp.concatenate(lhs, axis=0), wt1[...], preferred_element_type=F32) + bias_one
        side_pre[0, pl.ds(r0, 16), :] = pre[:16, :128]
        side_pre[1, pl.ds(r0, 16), :] = pre[-16:, 128:]
        h = elu(pre)
        parts = [h[16 * g : 16 * g + 16] for g in range(GROUPS)]
        for g, piece in enumerate(parts):
            hb[pl.ds(r0, 16), pl.ds(g * 256, 256)] = piece.astype(BF16)
        at_row = r0 + lax.broadcasted_iota(jnp.int32, (16, 128), 0)
        final = (at_row >= 2) & (at_row < ROWS - 2)
        for n, value in enumerate((parts[0][:, 128:], fold(parts[1:-1]), parts[-1][:, :128])):
            hs[n, pl.ds(r0, 16), :] = jnp.where(final, value, 0.0)
        cells = xe[pl.ds(EDGE + r0, 16), pl.ds(OWN, LANES)].astype(F32)
        xs[pl.ds(r0, 16), :] = functools.reduce(
            jnp.add, [cells[:, p * 128 : (p + 1) * 128] for p in range(PAIRS)]
        )

    for k in range(2):
        lhs = jnp.concatenate([expand(compact, 2 * k), expand(compact, 2 * k + 1)], axis=1)
        edge_pre[k] = (
            jnp.dot(lhs, wt1[pl.ds(512 * (1 - k), 1024), :], preferred_element_type=F32) + bias_one
        )

    combos = [(a, v) for a in range(3) for v in range(3)]
    at = lax.broadcasted_iota(jnp.int32, (16, 128), 1)
    which = lax.broadcasted_iota(jnp.int32, (16, 128), 0)
    own_at = by_row(at, 0)
    pick = jnp.zeros((16, 128), F32)
    for k, (a, v) in enumerate(combos):
        pick = jnp.where(which == k, by_row(at - 4 * (a - 1), v), pick)
    pick = pick * own_at
    inside = jnp.where((at >= 2) & (at < ROWS - 2), pick, 0.0)
    weights = jnp.concatenate([inside, jnp.where(which == 9, own_at, 0.0)], axis=1).astype(BF16)
    pick = pick.astype(BF16)
    for g in range(GROUPS):
        cells = jnp.concatenate(
            [hb[:, pl.ds(g * 256, 256)], xe[pl.ds(EDGE, ROWS), pl.ds(OWN + g * 256, 256)]], axis=0
        )
        sums = jnp.dot(weights, cells, preferred_element_type=F32)
        csum[pl.ds(g * 32, 16), :] = sums[:, :128]
        csum[pl.ds(g * 32 + 16, 16), :] = sums[:, 128:]
    cacc[...] = jnp.zeros_like(cacc)
    cacc[pl.ds(8, PAIRS), :] = csum[pl.ds(9, PAIRS, stride=16), :] + bias_two * (
        64.0 * (mt[1][0] + mt[2][0])
    )

    i = lax.broadcasted_iota(jnp.int32, (112, 128), 0)
    j = lax.broadcasted_iota(jnp.int32, (112, 128), 1)
    lower = j // 64
    pair_at = j % 32 // 2 * 2 + j // 32 % 2
    by_column = (lower == i // 32) & (pair_at == i % 32) & (pair_at > 0) & (pair_at < PAIRS - 1)
    kind = (i - 64) // 16
    in_kind = ((kind == 0) & (pair_at >= 2) & (pair_at < PAIRS - 2)) | (
        (kind > 0) & (pair_at == jnp.where(kind == 1, 1, PAIRS - 2))
    )
    by_line = in_kind & (lower == (i // 8) % 2) & (j % 2 + 6 * lower == i % 8)
    gather[...] = jnp.where(((i < 64) & by_column) | ((i >= 64) & by_line), 1.0, 0.0).astype(BF16)

    for copy in copies:
        copy.wait()

    @pl.when(r == 0)
    def _():
        side[:, low] = jnp.zeros((2, EDGE, 128), BF16)

    @pl.when(r == n_row - 1)
    def _():
        side[:, high] = jnp.zeros((2, EDGE, 128), BF16)

    edges = []
    for k, present in ((0, r > 0), (1, r < n_row - 1)):
        term = jnp.dot(expand(landed, k), wt1[pl.ds(1024 * k, 512), :], preferred_element_type=F32)
        edges.append(jnp.where(present, term, 0.0))
    line = lax.broadcasted_iota(jnp.int32, (8, 128), 0)
    flat = []
    for k, present in ((0, c > 0), (1, c < n_col - 1)):
        window = side[k]
        lhs = jnp.concatenate([window[14:142], window[16:144], window[18:146]], axis=1)
        taps = jnp.concatenate([wt1[pl.ds(a * 512 + 256 * k, 128), pl.ds(0, 128)] for a in range(3)], axis=0)
        term = jnp.dot(lhs, taps, preferred_element_type=F32)
        value = side_pre[k] + jnp.where(present, term, 0.0)
        if k == 0:
            head, tail = edges[0][:8, :128], pltpu.roll(edges[1][:8, :128], 6, 0)
        else:
            head, tail = pltpu.roll(edges[0][24:, 128:], 2, 0), edges[1][24:, 128:]
        value = jnp.concatenate(
            [
                value[:8] + jnp.where(line < 2, head, 0.0),
                value[8:120],
                value[120:] + jnp.where(line >= 6, tail, 0.0),
            ],
            axis=0,
        )
        flat.append(elu(value))
    sums = jnp.dot(
        pick, jnp.concatenate([v.astype(BF16) for v in flat], axis=1), preferred_element_type=F32
    )
    csum[pl.ds(0, 16), :] = sums[:, :128]
    csum[pl.ds(16 * (PAIRS - 1), 16), :] = sums[:, 128:]
    edges = [elu(edge_pre[k] + edges[k]).astype(BF16) for k in range(2)]
    cells = jnp.concatenate([edges[0][:, :128], edges[0][:, 128:], edges[1][:, :128], edges[1][:, 128:]], axis=0)
    found = jnp.dot(gather[...], cells, preferred_element_type=F32)

    def column(a, v):
        upper = mt[1][0] * (mt[0][v] if a == 2 else mt[1][v])
        under = mt[2][0] * (mt[3][v] if a == 0 else mt[2][v])
        return csum[pl.ds(3 * a + v, PAIRS, stride=16), :] + upper * found[:32] + under * found[32:64]

    at_pair = lax.broadcasted_iota(jnp.int32, (PAIRS, 128), 0)
    for b in range(3):
        pieces = []
        for a in range(3):
            value = column(a, 0)
            if b == 0:
                value = jnp.where(at_pair >= PAIRS - 2, column(a, 2), value)
            if b == 2:
                value = jnp.where(at_pair < 2, column(a, 1), value)
            pieces.append(value)
        weights = jnp.concatenate([wt2[pl.ds((a * 3 + b) * 128, 128), :] for a in range(3)], axis=0)
        both = jnp.dot(split(jnp.concatenate(pieces, axis=1)), weights, preferred_element_type=F32)
        cacc[pl.ds(8 - 2 * (b - 1), PAIRS), :] += both[:PAIRS] + both[PAIRS:]
    columns = cacc[pl.ds(4, 40), :]
    for k in range(10):
        csend[k] = columns[4 * k : 4 * k + 4]

    def post(src, dst, send_sem, recv_sem, tr, tc):
        mine = (tr == r) & (tc == c)

        @pl.when(mine)
        def _():
            pltpu.make_async_copy(src, dst, recv_sem).start()

        @pl.when(jnp.logical_not(mine))
        def _():
            pltpu.make_async_remote_copy(
                src_ref=src, dst_ref=dst, send_sem=send_sem, recv_sem=recv_sem, device_id=(tr, tc),
                device_id_type=MESH,
            ).start()

    def col_target(k):
        target = lax.rem(8 * c - 1 + k + n_all, n_all)
        return target // n_col, lax.rem(target, n_col)

    pl.semaphore_wait(ready, n_col - 1)
    for k in range(10):
        slot = r + n_row if k in (0, 9) else r
        post(csend.at[k], crecv.at[slot], col_send.at[k], col_recv.at[slot], *col_target(k))

    for k in range(2):
        hs[2 * k] += flat[k]
    for k, n in enumerate((1, 0, 2)):
        hs[n, pl.ds(0, 8), :] += found[64 + 16 * k : 72 + 16 * k]
        hs[n, pl.ds(ROWS - 8, 8), :] += found[72 + 16 * k : 80 + 16 * k]
    rows = lax.broadcasted_iota(jnp.int32, (ROWS, 128), 0)
    own = by_row(rows, 0)
    sum_l, sum_m, sum_r = (hs[k] * own for k in range(3))
    racc[...] = jnp.zeros_like(racc)
    racc[pl.ds(8, ROWS), :] = (xs[...] + 32.0 * bias_two) * own
    for a in range(3):
        out_rows = rows - 4 * (a - 1)
        m0, ml, mr = (by_row(out_rows, v) for v in range(3))
        lhs = split(
            jnp.concatenate(
                [
                    m0 * (sum_l + sum_m) + mr * sum_r,
                    m0 * (sum_l + sum_m + sum_r),
                    m0 * (sum_m + sum_r) + ml * sum_l,
                ],
                axis=1,
            )
        )
        both = jnp.dot(lhs, wt2[pl.ds(a * 384, 384), :], preferred_element_type=F32)
        racc[pl.ds(8 - 4 * (a - 1), ROWS), :] += both[:ROWS] + both[ROWS:]
    racc[...] = racc[...] + pltpu.roll(racc[...], 64, 1)
    half = lax.broadcasted_iota(jnp.int32, (72, 128), 1) < 64
    paired = jnp.where(half, racc[pl.ds(0, 72, stride=2), :], racc[pl.ds(1, 72, stride=2), :])
    for k in range(18):
        rsend[k] = paired[4 * k : 4 * k + 4]


    rrecv[c] = rsend[c + 1]
    for k in range(1, n_col):
        tc = lax.rem(c + k, n_col)
        pltpu.make_async_remote_copy(
            src_ref=rsend.at[tc + 1], dst_ref=rrecv.at[c], send_sem=row_send.at[k], recv_sem=row_recv.at[c],
            device_id=(r, tc), device_id_type=MESH,
        ).start()
    for k, tr, tc in ((0, up, n_col - 1), (17, down, 0)):
        pltpu.make_async_remote_copy(
            src_ref=rsend.at[k], dst_ref=rrecv.at[n_col + c], send_sem=row_send.at[k],
            recv_sem=row_recv.at[n_col + c], device_id=(tr, tc), device_id_type=MESH,
        ).start()

    def arrived(buffer, sem, slot):
        pltpu.make_async_copy(buffer.at[slot], buffer.at[slot], sem.at[slot]).wait()

    for k in range(1, n_col):
        arrived(rrecv, row_recv, lax.rem(c + k, n_col))

    @pl.when(row_edge)
    def _():
        for k in range(n_col):
            arrived(rrecv, row_recv, n_col + k)

    for k in range(n_row):
        arrived(crecv, col_recv, k)

    @pl.when(col_edge)
    def _():
        for k in range(n_row):
            arrived(crecv, col_recv, n_row + k)

    sums = jnp.sum(rrecv[...], axis=0) + jnp.sum(crecv[...], axis=0)
    res[pl.ds(0, 4, stride=2), :] = sums
    res[pl.ds(1, 4, stride=2), :] = pltpu.roll(sums, 64, 1)
    pooled = res[:, :64]
    center = jnp.mean(pooled, axis=1, keepdims=True)
    spread = jnp.mean((pooled - center) ** 2, axis=1, keepdims=True)
    normed = ((pooled - center) / jnp.sqrt(spread + EPSILON) * gain[...]).astype(BF16)
    out[...] = jnp.dot(normed, wp[...], preferred_element_type=F32).astype(BF16)

    for k in range(18):
        if k != n_col:
            pltpu.make_async_copy(rsend.at[k], rsend.at[k], row_send.at[k]).wait()
    for k in range(10):
        tr, tc = col_target(k)

        @pl.when((tr != r) | (tc != c))
        def _():
            pltpu.make_async_copy(csend.at[k], csend.at[k], col_send.at[k]).wait()


def body(pair, tile_mask, w_first, b_first, w_second, b_second, norm_gain, w_proj):
    n_row, n_col = lax.axis_size("row"), lax.axis_size("col")
    hbm = pl.BlockSpec(memory_space=pltpu.HBM)
    return pl.pallas_call(
        functools.partial(kernel, n_row, n_col),
        out_shape=pltpu.VMEM((8, w_proj.shape[1]), BF16),
        in_specs=[hbm] * 8,
        out_specs=pl.BlockSpec(memory_space=pltpu.VMEM),
        scratch_shapes=[
            pltpu.SMEM(tile_mask.shape, jnp.int32),
            pltpu.VMEM(w_first.shape, BF16),
            pltpu.VMEM((1, 64), F32),
            pltpu.VMEM(w_second.shape, BF16),
            pltpu.VMEM((1, 64), F32),
            pltpu.VMEM((1, 64), F32),
            pltpu.VMEM(w_proj.shape, BF16),
            pltpu.VMEM((ROWS + 2 * EDGE, LANES + 256), BF16),
            pltpu.VMEM((16, LANES + 256), BF16),
            pltpu.VMEM((16, LANES + 256), BF16),
            pltpu.VMEM((ROWS, LANES), BF16),
            pltpu.VMEM((1536, 256), BF16),
            pltpu.VMEM((1152, 128), BF16),
            pltpu.VMEM((3, ROWS, 128), F32),
            pltpu.VMEM((ROWS, 128), F32),
            pltpu.VMEM((144, 128), F32),
            pltpu.VMEM((48, 128), F32),
            pltpu.VMEM((512, 128), F32),
            pltpu.VMEM((4, 64, 256), BF16),
            pltpu.VMEM((2, 64, 256), BF16),
            pltpu.VMEM((2, ROWS + 2 * EDGE, 128), BF16),
            pltpu.VMEM((2, ROWS, 128), F32),
            pltpu.VMEM((2, 32, 256), F32),
            pltpu.VMEM((112, 128), BF16),
            pltpu.VMEM((18, 4, 128), F32),
            pltpu.VMEM((10, 4, 128), F32),
            pltpu.VMEM((32, 4, 128), F32),
            pltpu.VMEM((16, 4, 128), F32),
            pltpu.VMEM((8, 128), F32),
            pltpu.SemaphoreType.REGULAR,
            pltpu.SemaphoreType.DMA((3,)),
            pltpu.SemaphoreType.DMA((7,)),
            pltpu.SemaphoreType.DMA((8,)),
            pltpu.SemaphoreType.DMA((8,)),
            pltpu.SemaphoreType.DMA((18,)),
            pltpu.SemaphoreType.DMA((32,)),
            pltpu.SemaphoreType.DMA((10,)),
            pltpu.SemaphoreType.DMA((16,)),
        ],
        compiler_params=pltpu.CompilerParams(
            collective_id=0, has_side_effects=True, vmem_limit_bytes=48 * 1024 * 1024
        ),
        name="block",
    )(
        *(pltpu.with_memory_space_constraint(v, pltpu.HBM) for v in (
        pair, tile_mask, w_first, b_first.reshape(1, -1), w_second, b_second.reshape(1, -1),
        norm_gain.reshape(1, -1), w_proj,
    )))


def solution(mesh):
    return jax.shard_map(
        body,
        mesh=mesh,
        in_specs=(P("row", "col"), P(), P(), P(), P(), P(), P(), P()),
        out_specs=P(("row", "col"), None),
        check_vma=False,
    )
```

time: 23.8 us -> 21.7 us (0.912)
  Pallas kernels: 23 us -> 20.9 us
    pallas_call x1, Pallas kernels: 23 us -> 20.9 us  [body(): pl.pallas_call(functools.partial(kernel, n_row, n_col), out_shape=pltpu.V...]
where the time goes in v5:
time: 21.7 us; the launch traced here: 21.5 us
  Pallas kernels  20.9 us (96%)
  local copies, waits for them, and re-layouts  0.6 us (3%)
    pallas_call x1, Pallas kernels, body(): pl.pallas_call(functools.partial(kernel, n_row, n_col), out_shape=pltpu.V...  20.9 us
    unnamed x1, local copies, waits for them, and re-layouts  0.6 us

profile of v5, /device:TPU:0, one launch (start us, length us, event | category | flops | bytes accessed | tf_op | source)
XLA Modules:
  0.0 21.5 jit_solution(14398348786884074433)
XLA Ops:
  0.0 20.9 %block.1 = bf16[8,384]{1,0:T(8,128)(2,1)S(1)} custom-call(bf16[128,4096]{1,0:T(8,128)(2,1)} %pair.1, s32[16,16]{1,0:T(8,128)} %mask_in.1, bf16[3,3,64,64]{3,2,1,0:T(8,128)(2,1)} %w1_in.1, f32[1,64]{1,0:T(1,128)} %bitcast.3, bf16[3,3,64,64]{3,2,1,0:T(8,128)(2,1)} %w2_in.1, f32[1,64]{1,0:T(1,128)} %bitcast.4, f32[1,64]{1,0:T(1,128)} %bitcast.5, ...), custom_call_target="tpu_custom_call" | custom-call | tf_op jit(solution)/shard_map/block/pallas_call | solution.py:421
  20.9 0.6 %copy.10 = bf16[8,384]{1,0:T(8,128)(2,1)} copy(bf16[8,384]{1,0:T(8,128)(2,1)S(1)} %block.1) | data formatting | bytes 12288

commit v6 on v5

--- a/solution.py
+++ b/solution.py
@@ -59,20 +59,24 @@
     first, last = pl.ds(OWN, 128), pl.ds(OWN + LANES - 128, 128)
     top, bottom = pl.ds(EDGE, EDGE), pl.ds(ROWS, EDGE)
     inner, low, high = pl.ds(EDGE, ROWS), pl.ds(0, EDGE), pl.ds(EDGE + ROWS, EDGE)
+    has_up, has_down, has_left, has_right = r > 0, r < n_row - 1, c > 0, c < n_col - 1
     halos = [
-        (up, c, compact.at[0, pl.ds(16, 32)], landed.at[1, pl.ds(16, 32)]),
-        (down, c, compact.at[3, pl.ds(16, 32)], landed.at[0, pl.ds(16, 32)]),
-        (r, left, xe.at[whole, first], side.at[1, inner]),
-        (r, right, xe.at[whole, last], side.at[0, inner]),
-        (up, left, xe.at[top, first], side.at[1, high]),
-        (up, right, xe.at[top, last], side.at[0, high]),
-        (down, left, xe.at[bottom, first], side.at[1, low]),
-        (down, right, xe.at[bottom, last], side.at[0, low]),
+        (has_up, up, c, compact.at[0, pl.ds(16, 32)], landed.at[1, pl.ds(16, 32)]),
+        (has_down, down, c, compact.at[3, pl.ds(16, 32)], landed.at[0, pl.ds(16, 32)]),
+        (has_left, r, left, xe.at[whole, first], side.at[1, inner]),
+        (has_right, r, right, xe.at[whole, last], side.at[0, inner]),
+        (has_up & has_left, up, left, xe.at[top, first], side.at[1, high]),
+        (has_up & has_right, up, right, xe.at[top, last], side.at[0, high]),
+        (has_down & has_left, down, left, xe.at[bottom, first], side.at[1, low]),
+        (has_down & has_right, down, right, xe.at[bottom, last], side.at[0, low]),
     ]
     for k in range(1, n_row):
         greet(barrier, lax.rem(r + k, n_row), c)
-    for halo in halos[4:]:
-        greet(barrier, halo[0], halo[1])
+    for present, tr, tc, _, _ in halos[4:]:
+        @pl.when(present)
+        def _():
+            greet(barrier, tr, tc)
+
     for k in range(1, n_col):
         greet(barrier, r, lax.rem(c + k, n_col))
     for copy in loads + small:
@@ -90,8 +94,19 @@
         compact[k, pl.ds(0, 16), :] = jnp.zeros((16, 256), BF16)
         compact[k, pl.ds(48, 16), :] = jnp.zeros((16, 256), BF16)
 
-    row_edge = (c == 0) | (c == n_col - 1)
-    col_edge = (part == 0) | (part == 7)
+    for k, present, place in ((0, has_up, low), (1, has_down, high)):
+        @pl.when(jnp.logical_not(present))
+        def _():
+            landed[k, pl.ds(16, 32), :] = jnp.zeros((32, 256), BF16)
+            side[:, place] = jnp.zeros((2, EDGE, 128), BF16)
+
+    for k, present in ((0, has_left), (1, has_right)):
+        @pl.when(jnp.logical_not(present))
+        def _():
+            side[k] = jnp.zeros((ROWS + 2 * EDGE, 128), BF16)
+
+    row_edge = ((c == 0) & has_up) | ((c == n_col - 1) & has_down)
+    col_edge = ((part == 0) & (me > 0)) | ((part == 7) & (me < n_all - 1))
 
     @pl.when(jnp.logical_not(row_edge))
     def _():
@@ -115,16 +130,23 @@
         compact[2 * k + 1, pl.ds(16, 32), :] = both[32:]
 
     loads[2].wait()
-    pl.semaphore_wait(barrier, (n_row - 1) + 4 + (n_col - 1))
+    corners = (has_up.astype(jnp.int32) + has_down.astype(jnp.int32)) * (
+        has_left.astype(jnp.int32) + has_right.astype(jnp.int32)
+    )
+    pl.semaphore_wait(barrier, (n_row - 1) + (n_col - 1) + corners)
     copies = []
     for k in (0, 1, 4, 5, 6, 7, 2, 3):
-        tr, tc, src, dst = halos[k]
+        present, tr, tc, src, dst = halos[k]
         copy = pltpu.make_async_remote_copy(
             src_ref=src, dst_ref=dst, send_sem=halo_send.at[k], recv_sem=halo_recv.at[k],
             device_id=(tr, tc), device_id_type=MESH,
         )
-        copy.start()
-        copies.append(copy)
+        copies.append((present, k, copy))
+
+        @pl.when(present)
+        def _():
+            copy.start()
+
     for k in range(1, n_col):
         greet(ready, r, lax.rem(c + k, n_col))
 
@@ -241,29 +263,24 @@
     by_line = in_kind & (lower == (i // 8) % 2) & (j % 2 + 6 * lower == i % 8)
     gather[...] = jnp.where(((i < 64) & by_column) | ((i >= 64) & by_line), 1.0, 0.0).astype(BF16)
 
-    for copy in copies:
-        copy.wait()
-
-    @pl.when(r == 0)
-    def _():
-        side[:, low] = jnp.zeros((2, EDGE, 128), BF16)
-
-    @pl.when(r == n_row - 1)
-    def _():
-        side[:, high] = jnp.zeros((2, EDGE, 128), BF16)
+    sender = (has_down, has_up, has_right, has_left, has_down & has_right, has_down & has_left,
+              has_up & has_right, has_up & has_left)
+    for _, k, copy in copies:
+        @pl.when(sender[k])
+        def _():
+            copy.wait_recv()
 
     edges = []
-    for k, present in ((0, r > 0), (1, r < n_row - 1)):
-        term = jnp.dot(expand(landed, k), wt1[pl.ds(1024 * k, 512), :], preferred_element_type=F32)
-        edges.append(jnp.where(present, term, 0.0))
+    for k in range(2):
+        edges.append(jnp.dot(expand(landed, k), wt1[pl.ds(1024 * k, 512), :], preferred_element_type=F32))
     line = lax.broadcasted_iota(jnp.int32, (8, 128), 0)
     flat = []
-    for k, present in ((0, c > 0), (1, c < n_col - 1)):
+    for k in range(2):
         window = side[k]
         lhs = jnp.concatenate([window[14:142], window[16:144], window[18:146]], axis=1)
         taps = jnp.concatenate([wt1[pl.ds(a * 512 + 256 * k, 128), pl.ds(0, 128)] for a in range(3)], axis=0)
         term = jnp.dot(lhs, taps, preferred_element_type=F32)
-        value = side_pre[k] + jnp.where(present, term, 0.0)
+        value = side_pre[k] + term
         if k == 0:
             head, tail = edges[0][:8, :128], pltpu.roll(edges[1][:8, :128], 6, 0)
         else:
@@ -327,9 +344,14 @@
         return target // n_col, lax.rem(target, n_col)
 
     pl.semaphore_wait(ready, n_col - 1)
-    for k in range(10):
-        slot = r + n_row if k in (0, 9) else r
-        post(csend.at[k], crecv.at[slot], col_send.at[k], col_recv.at[slot], *col_target(k))
+    for k in range(1, 9):
+        post(csend.at[k], crecv.at[r], col_send.at[k], col_recv.at[r], *col_target(k))
+    for k, present in ((0, has_left), (9, has_right)):
+        @pl.when(present)
+        def _():
+            post(
+                csend.at[k], crecv.at[n_row + r], col_send.at[k], col_recv.at[n_row + r], *col_target(k)
+            )
 
     for k in range(2):
         hs[2 * k] += flat[k]
@@ -363,17 +385,20 @@
         rsend[k] = paired[4 * k : 4 * k + 4]
 
 
+    for k, present, tr, tc in ((0, has_up, up, n_col - 1), (17, has_down, down, 0)):
+        @pl.when(present)
+        def _():
+            pltpu.make_async_remote_copy(
+                src_ref=rsend.at[k], dst_ref=rrecv.at[n_col + c], send_sem=row_send.at[k],
+                recv_sem=row_recv.at[n_col + c], device_id=(tr, tc), device_id_type=MESH,
+            ).start()
+
     rrecv[c] = rsend[c + 1]
     for k in range(1, n_col):
         tc = lax.rem(c + k, n_col)
         pltpu.make_async_remote_copy(
             src_ref=rsend.at[tc + 1], dst_ref=rrecv.at[c], send_sem=row_send.at[k], recv_sem=row_recv.at[c],
             device_id=(r, tc), device_id_type=MESH,
-        ).start()
-    for k, tr, tc in ((0, up, n_col - 1), (17, down, 0)):
-        pltpu.make_async_remote_copy(
-            src_ref=rsend.at[k], dst_ref=rrecv.at[n_col + c], send_sem=row_send.at[k],
-            recv_sem=row_recv.at[n_col + c], device_id=(tr, tc), device_id_type=MESH,
         ).start()
 
     def arrived(buffer, sem, slot):
@@ -404,13 +429,21 @@
     normed = ((pooled - center) / jnp.sqrt(spread + EPSILON) * gain[...]).astype(BF16)
     out[...] = jnp.dot(normed, wp[...], preferred_element_type=F32).astype(BF16)
 
+    for present, _, copy in copies:
+        @pl.when(present)
+        def _():
+            copy.wait_send()
+
     for k in range(18):
         if k != n_col:
-            pltpu.make_async_copy(rsend.at[k], rsend.at[k], row_send.at[k]).wait()
+            @pl.when(has_up if k == 0 else has_down if k == 17 else r >= 0)
+            def _():
+                pltpu.make_async_copy(rsend.at[k], rsend.at[k], row_send.at[k]).wait()
+
     for k in range(10):
         tr, tc = col_target(k)
 
-        @pl.when((tr != r) | (tc != c))
+        @pl.when((has_left if k == 0 else has_right if k == 9 else r >= 0) & ((tr != r) | (tc != c)))
         def _():
             pltpu.make_async_copy(csend.at[k], csend.at[k], col_send.at[k]).wait()
 

time: 21.7 us -> 20.3 us (0.935)
  the two profiles are of different devices: /device:TPU:0 before, /device:TPU:1 now
where the time goes in v6:
time: 20.3 us; the launch traced here: 20.2 us
  Pallas kernels  19.6 us (97%)
  local copies, waits for them, and re-layouts  0.6 us (3%)
    pallas_call x1, Pallas kernels, body(): pl.pallas_call(functools.partial(kernel, n_row, n_col), out_shape=pltpu.V...  19.6 us
    unnamed x1, local copies, waits for them, and re-layouts  0.6 us

profile of v6, /device:TPU:1, one launch (start us, length us, event | category | flops | bytes accessed | tf_op | source)
XLA Modules:
  0.0 20.2 jit_solution(269943621651121878)
XLA Ops:
  0.0 19.6 %block.1 = bf16[8,384]{1,0:T(8,128)(2,1)S(1)} custom-call(bf16[128,4096]{1,0:T(8,128)(2,1)} %pair.1, s32[16,16]{1,0:T(8,128)} %mask_in.1, bf16[3,3,64,64]{3,2,1,0:T(8,128)(2,1)} %w1_in.1, f32[1,64]{1,0:T(1,128)} %bitcast.3, bf16[3,3,64,64]{3,2,1,0:T(8,128)(2,1)} %w2_in.1, f32[1,64]{1,0:T(1,128)} %bitcast.4, f32[1,64]{1,0:T(1,128)} %bitcast.5, ...), custom_call_target="tpu_custom_call" | custom-call | tf_op jit(solution)/shard_map/block/pallas_call | solution.py:454
  19.6 0.6 %copy.10 = bf16[8,384]{1,0:T(8,128)(2,1)} copy(bf16[8,384]{1,0:T(8,128)(2,1)S(1)} %block.1) | data formatting | bytes 12288

commit v7 on v6

--- a/solution.py
+++ b/solution.py
@@ -19,6 +19,7 @@
 GROUPS = 16
 OWN = 128
 LANES = PAIRS * 128
+SPLIT = 4
 
 
 def elu(v):
@@ -30,7 +31,7 @@
     pair, mask_in, w1_in, b1_in, w2_in, b2_in, gain_in, wp_in,
     out,
     mask, w1, b1, w2, b2, gain, wp, xe, xm, xp, hb, wt1, wt2, hs, xs, racc, cacc, csum, compact, landed, side, side_pre, edge_pre, gather, rsend, csend, rrecv, crecv, res,
-    ready, load_sem, small_sem, halo_send, halo_recv, row_send, row_recv, col_send, col_recv,
+    ready, known, load_sem, small_sem, halo_send, halo_recv, row_send, row_recv, col_send, col_recv,
 ):
     r = lax.axis_index("row")
     c = lax.axis_index("col")
@@ -70,15 +71,16 @@
         (has_down & has_left, down, left, xe.at[bottom, first], side.at[1, low]),
         (has_down & has_right, down, right, xe.at[bottom, last], side.at[0, low]),
     ]
-    for k in range(1, n_row):
-        greet(barrier, lax.rem(r + k, n_row), c)
-    for present, tr, tc, _, _ in halos[4:]:
+    near = (lax.rem(r + 2, n_row), lax.rem(r + n_row - 2, n_row))
+    for present, tr, tc, _, _ in halos[:2] + halos[4:]:
         @pl.when(present)
         def _():
             greet(barrier, tr, tc)
 
-    for k in range(1, n_col):
+    for k in (8, 7, 9, 6, 10, 5, 11, 4, 12, 3, 13, 2, 14, 1, 15):
         greet(barrier, r, lax.rem(c + k, n_col))
+    for tr in near:
+        greet(barrier, tr, c)
     for copy in loads + small:
         copy.start()
     part = lax.rem(me, 8)
@@ -130,10 +132,9 @@
         compact[2 * k + 1, pl.ds(16, 32), :] = both[32:]
 
     loads[2].wait()
-    corners = (has_up.astype(jnp.int32) + has_down.astype(jnp.int32)) * (
-        has_left.astype(jnp.int32) + has_right.astype(jnp.int32)
-    )
-    pl.semaphore_wait(barrier, (n_row - 1) + (n_col - 1) + corners)
+    beside = has_up.astype(jnp.int32) + has_down.astype(jnp.int32)
+    corners = beside * (has_left.astype(jnp.int32) + has_right.astype(jnp.int32))
+    pl.semaphore_wait(barrier, (n_col - 1) + beside + len(near) + corners)
     copies = []
     for k in (0, 1, 4, 5, 6, 7, 2, 3):
         present, tr, tc, src, dst = halos[k]
@@ -147,8 +148,13 @@
         def _():
             copy.start()
 
-    for k in range(1, n_col):
-        greet(ready, r, lax.rem(c + k, n_col))
+    for present, tr, tc, _, _ in halos[:2]:
+        @pl.when(present)
+        def _():
+            greet(known, tr, tc)
+
+    for tr in near:
+        greet(known, tr, c)
 
     for copy in small:
         copy.wait()
@@ -196,8 +202,7 @@
         high_part = values.astype(BF16)
         return jnp.concatenate([high_part, (values - high_part.astype(F32)).astype(BF16)], axis=0)
 
-    @pl.loop(0, ROWS // 16)
-    def _(k):
+    def rows_of(k):
         r0 = pl.multiple_of(16 * k, 16)
         window = xe[pl.ds(r0, 48), :]
         xm[...] = window[14:30]
@@ -222,6 +227,21 @@
             jnp.add, [cells[:, p * 128 : (p + 1) * 128] for p in range(PAIRS)]
         )
 
+    pl.loop(0, SPLIT)(rows_of)
+
+    pl.semaphore_wait(known, len(near) + beside)
+    odd = lax.rem(c, 2)
+    owner_row, edge_row = c // 2, c // 2 - 1 + 2 * odd
+    edge_exists = (edge_row >= 0) & (edge_row < n_row)
+
+    for n, tells in ((0, r == owner_row), (1, edge_exists & (r == edge_row))):
+        @pl.when(tells)
+        def _():
+            for k in range(1, n_row):
+                greet(ready.at[n], lax.rem(r + k, n_row), c)
+
+    pl.loop(SPLIT, ROWS // 16)(rows_of)
+
     for k in range(2):
         lhs = jnp.concatenate([expand(compact, 2 * k), expand(compact, 2 * k + 1)], axis=1)
         edge_pre[k] = (
@@ -343,7 +363,11 @@
         target = lax.rem(8 * c - 1 + k + n_all, n_all)
         return target // n_col, lax.rem(target, n_col)
 
-    pl.semaphore_wait(ready, n_col - 1)
+    for k, told in ((0, r != owner_row), (1, edge_exists & (r != edge_row))):
+        @pl.when(told)
+        def _():
+            pl.semaphore_wait(ready.at[k], 1)
+
     for k in range(1, 9):
         post(csend.at[k], crecv.at[r], col_send.at[k], col_recv.at[r], *col_target(k))
     for k, present in ((0, has_left), (9, has_right)):
@@ -486,6 +510,7 @@
             pltpu.VMEM((32, 4, 128), F32),
             pltpu.VMEM((16, 4, 128), F32),
             pltpu.VMEM((8, 128), F32),
+            pltpu.SemaphoreType.REGULAR((2,)),
             pltpu.SemaphoreType.REGULAR,
             pltpu.SemaphoreType.DMA((3,)),
             pltpu.SemaphoreType.DMA((7,)),

time: 20.3 us -> 20.2 us (level)
  no operation moved by 1% of the time
where the time goes in v7:
time: 20.2 us; the launch traced here: 20.1 us
  Pallas kernels  19.5 us (97%)
  local copies, waits for them, and re-layouts  0.6 us (3%)
    pallas_call x1, Pallas kernels, body(): pl.pallas_call(functools.partial(kernel, n_row, n_col), out_shape=pltpu.V...  19.5 us
    unnamed x1, local copies, waits for them, and re-layouts  0.6 us

profile of v7, /device:TPU:1, one launch (start us, length us, event | category | flops | bytes accessed | tf_op | source)
XLA Modules:
  0.0 20.1 jit_solution(4744258196295651758)
XLA Ops:
  0.0 19.5 %block.1 = bf16[8,384]{1,0:T(8,128)(2,1)S(1)} custom-call(bf16[128,4096]{1,0:T(8,128)(2,1)} %pair.1, s32[16,16]{1,0:T(8,128)} %mask_in.1, bf16[3,3,64,64]{3,2,1,0:T(8,128)(2,1)} %w1_in.1, f32[1,64]{1,0:T(1,128)} %bitcast.3, bf16[3,3,64,64]{3,2,1,0:T(8,128)(2,1)} %w2_in.1, f32[1,64]{1,0:T(1,128)} %bitcast.4, f32[1,64]{1,0:T(1,128)} %bitcast.5, ...), custom_call_target="tpu_custom_call" | custom-call | tf_op jit(solution)/shard_map/block/pallas_call | solution.py:478
  19.5 0.6 %copy.10 = bf16[8,384]{1,0:T(8,128)(2,1)} copy(bf16[8,384]{1,0:T(8,128)(2,1)S(1)} %block.1) | data formatting | bytes 12288

commit v8 on v7

--- a/solution.py
+++ b/solution.py
@@ -131,31 +131,6 @@
         compact[2 * k, pl.ds(16, 32), :] = both[:32]
         compact[2 * k + 1, pl.ds(16, 32), :] = both[32:]
 
-    loads[2].wait()
-    beside = has_up.astype(jnp.int32) + has_down.astype(jnp.int32)
-    corners = beside * (has_left.astype(jnp.int32) + has_right.astype(jnp.int32))
-    pl.semaphore_wait(barrier, (n_col - 1) + beside + len(near) + corners)
-    copies = []
-    for k in (0, 1, 4, 5, 6, 7, 2, 3):
-        present, tr, tc, src, dst = halos[k]
-        copy = pltpu.make_async_remote_copy(
-            src_ref=src, dst_ref=dst, send_sem=halo_send.at[k], recv_sem=halo_recv.at[k],
-            device_id=(tr, tc), device_id_type=MESH,
-        )
-        copies.append((present, k, copy))
-
-        @pl.when(present)
-        def _():
-            copy.start()
-
-    for present, tr, tc, _, _ in halos[:2]:
-        @pl.when(present)
-        def _():
-            greet(known, tr, tc)
-
-    for tr in near:
-        greet(known, tr, c)
-
     for copy in small:
         copy.wait()
 
@@ -190,9 +165,52 @@
             rows < 0, mt[0][v], jnp.where(rows < 64, mt[1][v], jnp.where(rows < 128, mt[2][v], mt[3][v]))
         )
 
+    i = lax.broadcasted_iota(jnp.int32, (112, 128), 0)
+    j = lax.broadcasted_iota(jnp.int32, (112, 128), 1)
+    lower = j // 64
+    pair_at = j % 32 // 2 * 2 + j // 32 % 2
+    by_column = (lower == i // 32) & (pair_at == i % 32) & (pair_at > 0) & (pair_at < PAIRS - 1)
+    kind = (i - 64) // 16
+    in_kind = ((kind == 0) & (pair_at >= 2) & (pair_at < PAIRS - 2)) | (
+        (kind > 0) & (pair_at == jnp.where(kind == 1, 1, PAIRS - 2))
+    )
+    by_line = in_kind & (lower == (i // 8) % 2) & (j % 2 + 6 * lower == i % 8)
+    gather[...] = jnp.where(((i < 64) & by_column) | ((i >= 64) & by_line), 1.0, 0.0).astype(BF16)
+
     def expand(buffer, k):
         window = buffer[k]
         return jnp.concatenate([window[14:46, 128:], window[16:48], window[18:50, :128]], axis=1)
+
+    for k in range(2):
+        lhs = jnp.concatenate([expand(compact, 2 * k), expand(compact, 2 * k + 1)], axis=1)
+        edge_pre[k] = (
+            jnp.dot(lhs, wt1[pl.ds(512 * (1 - k), 1024), :], preferred_element_type=F32) + bias_one
+        )
+
+    loads[2].wait()
+    beside = has_up.astype(jnp.int32) + has_down.astype(jnp.int32)
+    corners = beside * (has_left.astype(jnp.int32) + has_right.astype(jnp.int32))
+    pl.semaphore_wait(barrier, (n_col - 1) + beside + len(near) + corners)
+    copies = []
+    for k in (0, 1, 4, 5, 6, 7, 2, 3):
+        present, tr, tc, src, dst = halos[k]
+        copy = pltpu.make_async_remote_copy(
+            src_ref=src, dst_ref=dst, send_sem=halo_send.at[k], recv_sem=halo_recv.at[k],
+            device_id=(tr, tc), device_id_type=MESH,
+        )
+        copies.append((present, k, copy))
+
+        @pl.when(present)
+        def _():
+            copy.start()
+
+    for present, tr, tc, _, _ in halos[:2]:
+        @pl.when(present)
+        def _():
+            greet(known, tr, tc)
+
+    for tr in near:
+        greet(known, tr, c)
 
     def fold(parts):
         both = functools.reduce(jnp.add, parts)
@@ -242,12 +260,6 @@
 
     pl.loop(SPLIT, ROWS // 16)(rows_of)
 
-    for k in range(2):
-        lhs = jnp.concatenate([expand(compact, 2 * k), expand(compact, 2 * k + 1)], axis=1)
-        edge_pre[k] = (
-            jnp.dot(lhs, wt1[pl.ds(512 * (1 - k), 1024), :], preferred_element_type=F32) + bias_one
-        )
-
     combos = [(a, v) for a in range(3) for v in range(3)]
     at = lax.broadcasted_iota(jnp.int32, (16, 128), 1)
     which = lax.broadcasted_iota(jnp.int32, (16, 128), 0)
@@ -270,18 +282,6 @@
     cacc[pl.ds(8, PAIRS), :] = csum[pl.ds(9, PAIRS, stride=16), :] + bias_two * (
         64.0 * (mt[1][0] + mt[2][0])
     )
-
-    i = lax.broadcasted_iota(jnp.int32, (112, 128), 0)
-    j = lax.broadcasted_iota(jnp.int32, (112, 128), 1)
-    lower = j // 64
-    pair_at = j % 32 // 2 * 2 + j // 32 % 2
-    by_column = (lower == i // 32) & (pair_at == i % 32) & (pair_at > 0) & (pair_at < PAIRS - 1)
-    kind = (i - 64) // 16
-    in_kind = ((kind == 0) & (pair_at >= 2) & (pair_at < PAIRS - 2)) | (
-        (kind > 0) & (pair_at == jnp.where(kind == 1, 1, PAIRS - 2))
-    )
-    by_line = in_kind & (lower == (i // 8) % 2) & (j % 2 + 6 * lower == i % 8)
-    gather[...] = jnp.where(((i < 64) & by_column) | ((i >= 64) & by_line), 1.0, 0.0).astype(BF16)
 
     sender = (has_down, has_up, has_right, has_left, has_down & has_right, has_down & has_left,
               has_up & has_right, has_up & has_left)
@@ -409,6 +409,16 @@
         rsend[k] = paired[4 * k : 4 * k + 4]
 
 
+    rrecv[c] = rsend[c + 1]
+    for k in range(n_col):
+        @pl.when(c != k)
+        def _():
+            pltpu.make_async_remote_copy(
+                src_ref=rsend.at[k + 1], dst_ref=rrecv.at[c], send_sem=row_send.at[k + 1],
+                recv_sem=row_recv.at[c], device_id=(r, k), device_id_type=MESH,
+            ).start()
+
+
     for k, present, tr, tc in ((0, has_up, up, n_col - 1), (17, has_down, down, 0)):
         @pl.when(present)
         def _():
@@ -416,14 +426,6 @@
                 src_ref=rsend.at[k], dst_ref=rrecv.at[n_col + c], send_sem=row_send.at[k],
                 recv_sem=row_recv.at[n_col + c], device_id=(tr, tc), device_id_type=MESH,
             ).start()
-
-    rrecv[c] = rsend[c + 1]
-    for k in range(1, n_col):
-        tc = lax.rem(c + k, n_col)
-        pltpu.make_async_remote_copy(
-            src_ref=rsend.at[tc + 1], dst_ref=rrecv.at[c], send_sem=row_send.at[k], recv_sem=row_recv.at[c],
-            device_id=(r, tc), device_id_type=MESH,
-        ).start()
 
     def arrived(buffer, sem, slot):
         pltpu.make_async_copy(buffer.at[slot], buffer.at[slot], sem.at[slot]).wait()
@@ -459,10 +461,9 @@
             copy.wait_send()
 
     for k in range(18):
-        if k != n_col:
-            @pl.when(has_up if k == 0 else has_down if k == 17 else r >= 0)
-            def _():
-                pltpu.make_async_copy(rsend.at[k], rsend.at[k], row_send.at[k]).wait()
+        @pl.when(has_up if k == 0 else has_down if k == 17 else c != k - 1)
+        def _():
+            pltpu.make_async_copy(rsend.at[k], rsend.at[k], row_send.at[k]).wait()
 
     for k in range(10):
         tr, tc = col_target(k)

time: 20.2 us -> 19.8 us (0.980)
  Pallas kernels: 19.5 us -> 19.1 us
    pallas_call x1, Pallas kernels: 19.5 us -> 19.1 us  [body(): pl.pallas_call(functools.partial(kernel, n_row, n_col), out_shape=pltpu.V...]
where the time goes in v8:
time: 19.8 us; the launch traced here: 19.7 us
  Pallas kernels  19.1 us (96%)
  local copies, waits for them, and re-layouts  0.6 us (3%)
    pallas_call x1, Pallas kernels, body(): pl.pallas_call(functools.partial(kernel, n_row, n_col), out_shape=pltpu.V...  19.1 us
    unnamed x1, local copies, waits for them, and re-layouts  0.6 us

profile of v8, /device:TPU:1, one launch (start us, length us, event | category | flops | bytes accessed | tf_op | source)
XLA Modules:
  0.0 19.7 jit_solution(17470050443928227639)
XLA Ops:
  0.0 19.1 %block.1 = bf16[8,384]{1,0:T(8,128)(2,1)S(1)} custom-call(bf16[128,4096]{1,0:T(8,128)(2,1)} %pair.1, s32[16,16]{1,0:T(8,128)} %mask_in.1, bf16[3,3,64,64]{3,2,1,0:T(8,128)(2,1)} %w1_in.1, f32[1,64]{1,0:T(1,128)} %bitcast.3, bf16[3,3,64,64]{3,2,1,0:T(8,128)(2,1)} %w2_in.1, f32[1,64]{1,0:T(1,128)} %bitcast.4, f32[1,64]{1,0:T(1,128)} %bitcast.5, ...), custom_call_target="tpu_custom_call" | custom-call | tf_op jit(solution)/shard_map/block/pallas_call | solution.py:479
  19.1 0.6 %copy.10 = bf16[8,384]{1,0:T(8,128)(2,1)} copy(bf16[8,384]{1,0:T(8,128)(2,1)S(1)} %block.1) | data formatting | bytes 12288

commit v9 on v8

--- a/solution.py
+++ b/solution.py
@@ -188,6 +188,15 @@
         )
 
     loads[2].wait()
+
+    @pl.loop(0, ROWS // 16)
+    def _(k):
+        r0 = pl.multiple_of(16 * k, 16)
+        cells = xe[pl.ds(EDGE + r0, 16), pl.ds(OWN, LANES)].astype(F32)
+        xs[pl.ds(r0, 16), :] = functools.reduce(
+            jnp.add, [cells[:, p * 128 : (p + 1) * 128] for p in range(PAIRS)]
+        )
+
     beside = has_up.astype(jnp.int32) + has_down.astype(jnp.int32)
     corners = beside * (has_left.astype(jnp.int32) + has_right.astype(jnp.int32))
     pl.semaphore_wait(barrier, (n_col - 1) + beside + len(near) + corners)
@@ -240,10 +249,6 @@
         final = (at_row >= 2) & (at_row < ROWS - 2)
         for n, value in enumerate((parts[0][:, 128:], fold(parts[1:-1]), parts[-1][:, :128])):
             hs[n, pl.ds(r0, 16), :] = jnp.where(final, value, 0.0)
-        cells = xe[pl.ds(EDGE + r0, 16), pl.ds(OWN, LANES)].astype(F32)
-        xs[pl.ds(r0, 16), :] = functools.reduce(
-            jnp.add, [cells[:, p * 128 : (p + 1) * 128] for p in range(PAIRS)]
-        )
 
     pl.loop(0, SPLIT)(rows_of)
 

time: 19.8 us -> 19.8 us (level)
  no operation moved by 1% of the time
where the time goes in v9:
time: 19.8 us; the launch traced here: 19.7 us
  Pallas kernels  19 us (96%)
  local copies, waits for them, and re-layouts  0.6 us (3%)
    pallas_call x1, Pallas kernels, body(): pl.pallas_call(functools.partial(kernel, n_row, n_col), out_shape=pltpu.V...  19 us
    unnamed x1, local copies, waits for them, and re-layouts  0.6 us

profile of v9, /device:TPU:1, one launch (start us, length us, event | category | flops | bytes accessed | tf_op | source)
XLA Modules:
  0.0 19.7 jit_solution(13059008772985161181)
XLA Ops:
  0.0 19.0 %block.1 = bf16[8,384]{1,0:T(8,128)(2,1)S(1)} custom-call(bf16[128,4096]{1,0:T(8,128)(2,1)} %pair.1, s32[16,16]{1,0:T(8,128)} %mask_in.1, bf16[3,3,64,64]{3,2,1,0:T(8,128)(2,1)} %w1_in.1, f32[1,64]{1,0:T(1,128)} %bitcast.3, bf16[3,3,64,64]{3,2,1,0:T(8,128)(2,1)} %w2_in.1, f32[1,64]{1,0:T(1,128)} %bitcast.4, f32[1,64]{1,0:T(1,128)} %bitcast.5, ...), custom_call_target="tpu_custom_call" | custom-call | tf_op jit(solution)/shard_map/block/pallas_call | solution.py:484
  19.1 0.6 %copy.10 = bf16[8,384]{1,0:T(8,128)(2,1)} copy(bf16[8,384]{1,0:T(8,128)(2,1)S(1)} %block.1) | data formatting | bytes 12288

commit v10 on v9

--- a/solution.py
+++ b/solution.py
@@ -188,6 +188,28 @@
         )
 
     loads[2].wait()
+    combos = [(a, v) for a in range(3) for v in range(3)]
+    at = lax.broadcasted_iota(jnp.int32, (16, 128), 1)
+    which = lax.broadcasted_iota(jnp.int32, (16, 128), 0)
+    own_at = by_row(at, 0)
+    pick = jnp.zeros((16, 128), F32)
+    for k, (a, v) in enumerate(combos):
+        pick = jnp.where(which == k, by_row(at - 4 * (a - 1), v), pick)
+    pick = pick * own_at
+    inside = jnp.where((at >= 2) & (at < ROWS - 2), pick, 0.0)
+    inside = inside.astype(BF16)
+    pick = pick.astype(BF16)
+    for g in range(GROUPS):
+        sums = jnp.dot(
+            own_at.astype(BF16), xe[pl.ds(EDGE, ROWS), pl.ds(OWN + g * 256, 256)], preferred_element_type=F32
+        )
+        csum[pl.ds(g * 32, 16), :] = sums[:, :128]
+        csum[pl.ds(g * 32 + 16, 16), :] = sums[:, 128:]
+    cacc[...] = jnp.zeros_like(cacc)
+    cacc[pl.ds(8, PAIRS), :] = csum[pl.ds(0, PAIRS, stride=16), :] + bias_two * (
+        64.0 * (mt[1][0] + mt[2][0])
+    )
+
 
     @pl.loop(0, ROWS // 16)
     def _(k):
@@ -265,28 +287,10 @@
 
     pl.loop(SPLIT, ROWS // 16)(rows_of)
 
-    combos = [(a, v) for a in range(3) for v in range(3)]
-    at = lax.broadcasted_iota(jnp.int32, (16, 128), 1)
-    which = lax.broadcasted_iota(jnp.int32, (16, 128), 0)
-    own_at = by_row(at, 0)
-    pick = jnp.zeros((16, 128), F32)
-    for k, (a, v) in enumerate(combos):
-        pick = jnp.where(which == k, by_row(at - 4 * (a - 1), v), pick)
-    pick = pick * own_at
-    inside = jnp.where((at >= 2) & (at < ROWS - 2), pick, 0.0)
-    weights = jnp.concatenate([inside, jnp.where(which == 9, own_at, 0.0)], axis=1).astype(BF16)
-    pick = pick.astype(BF16)
     for g in range(GROUPS):
-        cells = jnp.concatenate(
-            [hb[:, pl.ds(g * 256, 256)], xe[pl.ds(EDGE, ROWS), pl.ds(OWN + g * 256, 256)]], axis=0
-        )
-        sums = jnp.dot(weights, cells, preferred_element_type=F32)
+        sums = jnp.dot(inside, hb[:, pl.ds(g * 256, 256)], preferred_element_type=F32)
         csum[pl.ds(g * 32, 16), :] = sums[:, :128]
         csum[pl.ds(g * 32 + 16, 16), :] = sums[:, 128:]
-    cacc[...] = jnp.zeros_like(cacc)
-    cacc[pl.ds(8, PAIRS), :] = csum[pl.ds(9, PAIRS, stride=16), :] + bias_two * (
-        64.0 * (mt[1][0] + mt[2][0])
-    )
 
     sender = (has_down, has_up, has_right, has_left, has_down & has_right, has_down & has_left,
               has_up & has_right, has_up & has_left)

time: 19.8 us -> 19.7 us (level)
  no operation moved by 1% of the time
where the time goes in v10:
time: 19.7 us; the launch traced here: 19.6 us
  Pallas kernels  19 us (96%)
  local copies, waits for them, and re-layouts  0.6 us (3%)
    pallas_call x1, Pallas kernels, body(): pl.pallas_call(functools.partial(kernel, n_row, n_col), out_shape=pltpu.V...  19 us
    unnamed x1, local copies, waits for them, and re-layouts  0.6 us

profile of v10, /device:TPU:1, one launch (start us, length us, event | category | flops | bytes accessed | tf_op | source)
XLA Modules:
  0.0 19.6 jit_solution(6977487777366075831)
XLA Ops:
  0.0 19.0 %block.1 = bf16[8,384]{1,0:T(8,128)(2,1)S(1)} custom-call(bf16[128,4096]{1,0:T(8,128)(2,1)} %pair.1, s32[16,16]{1,0:T(8,128)} %mask_in.1, bf16[3,3,64,64]{3,2,1,0:T(8,128)(2,1)} %w1_in.1, f32[1,64]{1,0:T(1,128)} %bitcast.3, bf16[3,3,64,64]{3,2,1,0:T(8,128)(2,1)} %w2_in.1, f32[1,64]{1,0:T(1,128)} %bitcast.4, f32[1,64]{1,0:T(1,128)} %bitcast.5, ...), custom_call_target="tpu_custom_call" | custom-call | tf_op jit(solution)/shard_map/block/pallas_call | solution.py:488
  19.0 0.6 %copy.10 = bf16[8,384]{1,0:T(8,128)(2,1)} copy(bf16[8,384]{1,0:T(8,128)(2,1)S(1)} %block.1) | data formatting | bytes 12288

commit v11 on v9

--- a/solution.py
+++ b/solution.py
@@ -19,7 +19,7 @@
 GROUPS = 16
 OWN = 128
 LANES = PAIRS * 128
-SPLIT = 4
+SPLIT = 5
 
 
 def elu(v):

time: 19.8 us -> 19.8 us (level)
  no operation moved by 1% of the time
where the time goes in v11:
time: 19.8 us; the launch traced here: 19.7 us
  Pallas kernels  19 us (96%)
  local copies, waits for them, and re-layouts  0.6 us (3%)
    pallas_call x1, Pallas kernels, body(): pl.pallas_call(functools.partial(kernel, n_row, n_col), out_shape=pltpu.V...  19 us
    unnamed x1, local copies, waits for them, and re-layouts  0.6 us

profile of v11, /device:TPU:1, one launch (start us, length us, event | category | flops | bytes accessed | tf_op | source)
XLA Modules:
  0.0 19.7 jit_solution(9125877879497256011)
XLA Ops:
  0.0 19.0 %block.1 = bf16[8,384]{1,0:T(8,128)(2,1)S(1)} custom-call(bf16[128,4096]{1,0:T(8,128)(2,1)} %pair.1, s32[16,16]{1,0:T(8,128)} %mask_in.1, bf16[3,3,64,64]{3,2,1,0:T(8,128)(2,1)} %w1_in.1, f32[1,64]{1,0:T(1,128)} %bitcast.3, bf16[3,3,64,64]{3,2,1,0:T(8,128)(2,1)} %w2_in.1, f32[1,64]{1,0:T(1,128)} %bitcast.4, f32[1,64]{1,0:T(1,128)} %bitcast.5, ...), custom_call_target="tpu_custom_call" | custom-call | tf_op jit(solution)/shard_map/block/pallas_call | solution.py:484
  19.1 0.6 %copy.10 = bf16[8,384]{1,0:T(8,128)(2,1)} copy(bf16[8,384]{1,0:T(8,128)(2,1)S(1)} %block.1) | data formatting | bytes 12288
